TPU v7x, 32 devices: a whole 2x2x4 slice. The times are simulated.
32 devices in a mesh: chan: 8 (over y, x, core), day: 4 (over z).
Axes of the slice: x: 2, y: 2, z: 4, core: 2. Of those that a mesh axis runs over, the one named last changes fastest.
Arguments:
- records: bfloat16 [4, 512, 4096], P('day', 'chan'), may hold values from -50 to 50
- filter_taps: bfloat16 [64], replicated, may hold values from -0.75 to 0.75
- window_offsets: int32 [4, 2], P('day'), may hold values from 0 to 3009, as said below
- pair_masks: int32 [3], replicated, may hold values from 1 to 7, as said below
Outputs:
- stacks: float32 [3, 65, 32768], P(None, None, ('chan', 'day'))
Inputs may be any that keep to these rules, and one draw needn't show every extreme that they name: `window_offsets`: in each day group one window ends at the record's last sample. `pair_masks`: the masks are distinct; 1 and 7 are among them.
All inputs are finite; a program needn't handle non-finite values.
Results may differ from a plain program's by a relative error of at most 0.0029.
Values may be sent and summed in bfloat16 or wider, within the bound.
No kernel may reach another device: no remote copies, remote signals or barrier semaphores. Data moves between devices by JAX's collectives and lax.ppermute only.
A program may use at most 64 MiB of HBM per device.

v0:
```python
import functools

import jax
import jax.numpy as jnp
from jax import lax
from jax.experimental import pallas as pl
from jax.experimental.pallas import tpu as pltpu
from jax.sharding import PartitionSpec as P

L = 1024
MAXLAG = 32
LAGS = 2 * MAXLAG + 1
FINE = 16
COARSE = 4
PAD = 1152
CUT = 1280
NT = (((1,), (1,)), ((), ()))


def vmem(shape=None):
    return pl.BlockSpec(memory_space=pltpu.VMEM)


def smem():
    return pl.BlockSpec(memory_space=pltpu.SMEM)


def whiten_kernel(off_ref, taps_ref, rec_ref, out_ref, wide_ref):
    chans, rec_len = rec_ref.shape[1], rec_ref.shape[2]
    taps = taps_ref[...].astype(jnp.float32)
    row = jnp.concatenate([taps, jnp.zeros((1, 384 - taps.shape[1]), jnp.float32)], axis=1)
    row = jnp.broadcast_to(row, (8, 384))
    bands = []
    wide_ref[...] = jnp.zeros_like(wide_ref)
    for w in range(2):
        start = off_ref[0, w]
        base = jnp.minimum((start // 128) * 128, rec_len - CUT)
        base = pl.multiple_of(base, 128)
        moved = pltpu.roll(row, start - base, 1)
        block = jnp.broadcast_to(moved[0:1], (128, 384))
        block = pltpu.roll(block, 0, 1, stride=1, stride_axis=0).astype(jnp.bfloat16)
        none = jnp.zeros((128, 128), jnp.bfloat16)
        bands.append(
            jnp.concatenate(
                [jnp.concatenate([block, none], axis=1), jnp.concatenate([none, block], axis=1)],
                axis=0,
            )
        )
        wide_ref[w, w * chans : (w + 1) * chans, :] = rec_ref[0, :, pl.ds(base, CUT)]
    parts = []
    for c in range(L // 256):
        part = lax.dot_general(
            bands[0], wide_ref[0, :, c * 256 : c * 256 + 512], NT, preferred_element_type=jnp.float32
        )
        part += lax.dot_general(
            bands[1], wide_ref[1, :, c * 256 : c * 256 + 512], NT, preferred_element_type=jnp.float32
        )
        parts.append(part)
    power = sum(jnp.sum(part * part, axis=0, keepdims=True) for part in parts) * (1.0 / L)
    scale = lax.rsqrt(power + 1e-06)
    for c, part in enumerate(parts):
        out_ref[c * 256 : (c + 1) * 256, :] = (part * scale).astype(jnp.bfloat16)


def prepare_kernel(days, white_ref, keep_ref, send_ref):
    chans = white_ref.shape[1] // 2
    share = chans // days
    bits = days.bit_length() - 1
    me = lax.axis_index("day")
    rows = lax.broadcasted_iota(jnp.int32, (2 * chans, 2 * chans), 0)
    cols = lax.broadcasted_iota(jnp.int32, (2 * chans, 2 * chans), 1)
    place = (rows % chans) // share
    slot = jnp.zeros_like(place)
    for b in range(bits):
        slot = slot + (((place >> b) & 1) << (bits - 1 - b))
    source = (rows // chans) * chans + (slot ^ me) * share + rows % share
    pick = (cols == source).astype(jnp.float32).astype(jnp.bfloat16)
    mine = lax.dot_general(pick, white_ref[...], NT, preferred_element_type=jnp.float32)
    mine = jnp.concatenate([mine, jnp.zeros((2 * chans, PAD - L), jnp.float32)], axis=1)
    half = chans // 2
    for p in range(FINE + 1):
        moved = (pltpu.roll(mine, p, 1) if p else mine).astype(jnp.bfloat16)
        for w in range(2):
            span = slice(w * PAD, (w + 1) * PAD)
            keep_ref[p * half : (p + 1) * half, span] = moved[w * chans : w * chans + half]
            send_ref[p * half : (p + 1) * half, span] = moved[w * chans + half : (w + 1) * chans]


def correlate_kernel(theirs_ref, keep_ref, send_ref, kept_ref, sent_ref, w_ref):
    theirs = theirs_ref[...].astype(jnp.float32)
    swapped = pltpu.roll(theirs, 64, 1)
    low = lax.broadcasted_iota(jnp.int32, (1, 128), 1) < 64
    zero = jnp.zeros((16, 128), jnp.float32)
    for w, (a, b) in enumerate(((theirs, swapped), (swapped, theirs))):
        first = jnp.concatenate([zero, zero, a, zero, zero, zero, zero], axis=0)
        second = jnp.concatenate([zero, b, zero, zero, zero, zero, zero], axis=0)
        both = jnp.where(low, first, second).astype(jnp.bfloat16)
        rows = both.shape[0]
        w_ref[w * PAD : w * PAD + rows, 0:128] = both
        w_ref[w * PAD + rows : (w + 1) * PAD, 0:128] = jnp.zeros((PAD - rows, 128), jnp.bfloat16)
        w_ref[w * PAD : w * PAD + rows - 32, 128:256] = both[32:]
        w_ref[w * PAD + rows - 32 : (w + 1) * PAD, 128:256] = jnp.zeros((PAD - rows + 32, 128), jnp.bfloat16)
    weights = w_ref[...]
    sent_ref[...] = jnp.dot(send_ref[...], weights, preferred_element_type=jnp.float32).astype(jnp.bfloat16)
    kept_ref[...] = jnp.dot(keep_ref[...], weights, preferred_element_type=jnp.float32)


def finish_kernel(share, norm, order_ref, *refs):
    ins, out_ref, s_ref = refs[:-2], refs[-2], refs[-1]
    low = lax.broadcasted_iota(jnp.int32, (1, 128), 1) < 64
    for k in range(len(ins) // 2):
        total = (ins[2 * k][...] + ins[2 * k + 1][...].astype(jnp.float32)) * norm
        s_ref[0] = total[:, 0:128]
        s_ref[1] = total[:, 128:256]
        r = order_ref[k]
        for pair in range(share // 2):
            for tile in range(COARSE // 2):
                one = s_ref[tile, pl.ds(2 * pair, FINE, stride=share), :]
                two = s_ref[tile, pl.ds(2 * pair + 1, FINE, stride=share), :]
                to = slice(pair * 128, pair * 128 + 128)
                q = 2 * tile * FINE
                out_ref[r, q : q + FINE, to] = jnp.where(low, one, pltpu.roll(two, 64, 1))
                out_ref[r, q + FINE : q + 2 * FINE, to] = jnp.where(low, pltpu.roll(one, 64, 1), two)
            one = s_ref[1, FINE * share + 2 * pair : FINE * share + 2 * pair + 1, :]
            two = s_ref[1, FINE * share + 2 * pair + 1 : FINE * share + 2 * pair + 2, :]
            out_ref[r, LAGS - 1 : LAGS, pair * 128 : pair * 128 + 128] = jnp.where(low, pltpu.roll(one, 64, 1), two)


def apart(value, axis, mask):
    return lax.ppermute(value, axis, [(s, s ^ mask) for s in range(lax.axis_size(axis))])


def local(records, filter_taps, window_offsets, pair_masks):
    chans = records.shape[1]
    blocks = lax.axis_size("chan")
    days = lax.axis_size("day")
    share = chans // days
    params = pltpu.CompilerParams(vmem_limit_bytes=40 * 1024 * 1024)
    white = pl.pallas_call(
        whiten_kernel,
        out_shape=jax.ShapeDtypeStruct((L, 2 * chans), jnp.bfloat16),
        in_specs=[smem(), vmem(), vmem()],
        out_specs=vmem(),
        scratch_shapes=[pltpu.VMEM((2, 2 * chans, CUT), jnp.bfloat16)],
        compiler_params=params,
    )(window_offsets, filter_taps.reshape(1, -1), records)

    last = blocks - 1
    third = pair_masks[0] ^ pair_masks[1] ^ pair_masks[2] ^ 1 ^ last
    near = apart(white, "chan", 1)
    if blocks == 8:
        along_x = apart(white, "chan", 2)
        along_y = apart(white, "chan", 4)
        far = apart(white, "chan", last)
        chip = third >> 1
        held = jnp.where(chip == 3, far, jnp.where(chip == 1, along_x, along_y))
        other = apart(held, "chan", 1)
        free = jnp.where((third == 2) | (third == 4), held, other)
    else:
        far = apart(white, "chan", last)
        free = white
        for bit in range(blocks.bit_length() - 1):
            free = jnp.where(((third >> bit) & 1) == 1, apart(free, "chan", 2**bit), free)
    order = jnp.stack([jnp.argmax(pair_masks == m).astype(jnp.int32) for m in (jnp.int32(1), jnp.int32(last), third)])

    half_rows = (FINE + 1) * chans // 2
    keep, send = pl.pallas_call(
        functools.partial(prepare_kernel, days),
        out_shape=[jax.ShapeDtypeStruct((half_rows, 2 * PAD), jnp.bfloat16)] * 2,
        in_specs=[vmem()],
        out_specs=[vmem()] * 2,
        compiler_params=params,
    )(white)

    def correlate(theirs):
        kept, sent = pl.pallas_call(
            correlate_kernel,
            out_shape=[
                jax.ShapeDtypeStruct((half_rows, 256), jnp.float32),
                jax.ShapeDtypeStruct((half_rows, 256), jnp.bfloat16),
            ],
            in_specs=[vmem()] * 3,
            out_specs=[vmem()] * 2,
            scratch_shapes=[pltpu.VMEM((2 * PAD, 256), jnp.bfloat16)],
            compiler_params=params,
        )(theirs, keep, send)
        shape = (FINE + 1, chans // 2, 256)
        return kept.reshape(shape), sent.reshape(shape)

    finals = []
    for theirs in (near, far, free):
        kept, sent = correlate(theirs)
        step = 1
        while step < days:
            came = apart(sent, "day", step)
            step *= 2
            if step < days:
                total = kept + came.astype(jnp.float32)
                half = total.shape[1] // 2
                kept = total[:, :half]
                sent = total[:, half:].astype(jnp.bfloat16)
        rows = (FINE + 1) * share
        finals += [kept.reshape(rows, 256), came.reshape(rows, 256)]

    day_total = records.shape[0] * days
    norm = float((day_total * window_offsets.shape[1] * L) ** -0.5)
    return pl.pallas_call(
        functools.partial(finish_kernel, share, norm),
        out_shape=jax.ShapeDtypeStruct((3, LAGS, share * chans), jnp.float32),
        in_specs=[smem()] + [vmem()] * 6,
        out_specs=vmem(),
        scratch_shapes=[pltpu.VMEM((2, (FINE + 1) * share, 128), jnp.float32)],
        compiler_params=params,
    )(order, *finals)


def solution(mesh):
    in_specs = (P("day", "chan", None), P(), P("day", None), P())
    out_specs = P(None, None, ("chan", "day"))
    return jax.shard_map(local, mesh=mesh, in_specs=in_specs, out_specs=out_specs, check_vma=False)
```

profile of v0, /device:TPU:0, one launch (start us, length us, event | category | flops | bytes accessed | tf_op | source)
XLA Modules:
  0.0 64.9 jit_solution(13610026174754444912)
XLA Ops:
  0.0 1.0 %copy-done.4 = bf16[1,64,4096]{2,1,0:T(8,128)(2,1)S(1)} copy-done((bf16[1,64,4096]{2,1,0:T(8,128)(2,1)S(1)}, bf16[1,64,4096]{2,1,0:T(8,128)(2,1)}, u32[]{:S(2)}) %copy-start.4) | copy-done | bytes 524312
  1.0 0.7 %copy-done.5 = s32[1,2]{1,0:T(1,128)S(1)} copy-done((s32[1,2]{1,0:T(1,128)S(1)}, s32[1,2]{1,0:T(1,128)}, u32[]{:S(2)}) %copy-start.5) | copy-done | bytes 32
  1.7 0.7 %copy-done.6 = bf16[64]{0:T(256)(128)(2,1)S(1)} copy-done((bf16[64]{0:T(256)(128)(2,1)S(1)}, bf16[64]{0:T(256)(128)(2,1)}, u32[]{:S(2)}) %copy-start.6) | copy-done | bytes 152
  2.4 1.4 %shard_map.46.white_ref = bf16[1024,128]{1,0:T(8,128)(2,1)S(1)} custom-call(s32[1,2]{1,0:T(1,128)S(1)} %copy-done.5, bf16[1,64]{1,0:T(2,128)(2,1)S(1)} %bitcast.26, bf16[1,64,4096]{2,1,0:T(8,128)(2,1)S(1)} %copy-done.4), custom_call_target="tpu_custom_call" | custom-call | tf_op jit(solution)/shard_map/pallas_call | solution.py:139
  3.8 3.4 %collective-permute-start.3 = (bf16[1024,128]{1,0:T(8,128)(2,1)S(1)}, bf16[1024,128]{1,0:T(8,128)(2,1)S(1)}, u32[]{:S(2)}, u32[]{:S(2)}) collective-permute-start(bf16[1024,128]{1,0:T(8,128)(2,1)S(1)} %shard_map.46.white_ref), channel_id=1, source_target_pairs={{0,28},{4,24},{8,20},{12,16},{16,12},{20,8},{24,4},{28,0},{1,29},{... | collective-permute-start | bytes 786440 | tf_op jit(solution)/shard_map/ppermute | solution.py:130
  7.2 0.5 collective-permute-start.6
  7.7 0.7 %collective-permute-start.7 = (bf16[1024,128]{1,0:T(8,128)(2,1)S(1)}, bf16[1024,128]{1,0:T(8,128)(2,1)S(1)}, u32[]{:S(2)}, u32[]{:S(2)}) collective-permute-start(bf16[1024,128]{1,0:T(8,128)(2,1)S(1)} %shard_map.46.white_ref), channel_id=1, source_target_pairs={{0,16},{4,20},{8,24},{12,28},{16,0},{20,4},{24,8},{28,12},{1,17},{... | collective-permute-start | bytes 786440 | tf_op jit(solution)/shard_map/ppermute | solution.py:130
  8.4 1.4 %fusion = (s32[1]{0:T(128)}, s32[1]{0:T(128)}, s32[1]{0:T(128)}) fusion(s32[3]{0:T(128)} %param.7), kind=kLoop, calls=%fused_computation.12 | loop fusion | bytes 24 | tf_op jit(solution)/shard_map/slice | solution.py:149
  11.7 2.2 %collective-permute-done.3.theirs_ref = bf16[1024,128]{1,0:T(8,128)(2,1)S(1)} collective-permute-done((bf16[1024,128]{1,0:T(8,128)(2,1)S(1)}, bf16[1024,128]{1,0:T(8,128)(2,1)S(1)}, u32[]{:S(2)}, u32[]{:S(2)}) %collective-permute-start.3) | collective-permute-done | bytes 262176 | tf_op jit(solution)/shard_map/ppermute | solution.py:130
  13.9 6.6 %collective-permute-done.6 = bf16[1024,128]{1,0:T(8,128)(2,1)S(1)} collective-permute-done((bf16[1024,128]{1,0:T(8,128)(2,1)S(1)}, bf16[1024,128]{1,0:T(8,128)(2,1)S(1)}, u32[]{:S(2)}, u32[]{:S(2)}) %collective-permute-start.6) | collective-permute-done | bytes 262176 | tf_op jit(solution)/shard_map/ppermute | solution.py:130
  20.7 1.3 %compare_reduce_fusion = (pred[]{:T(512)}, s32[]{:T(128)}) fusion(s32[3]{0:T(128)} %param.7, s32[]{:T(128)} %bitcast.2), kind=kLoop, calls=%fused_computation.8 | loop fusion | flops 17 | bytes 21 | tf_op jit(solution)/shard_map/local/reduce | solution.py:164
  22.0 1.4 %shard_map.47 = (bf16[544,2304]{1,0:T(8,128)(2,1)S(1)}, bf16[544,2304]{1,0:T(8,128)(2,1)S(1)}) custom-call(bf16[1024,128]{1,0:T(8,128)(2,1)S(1)} %shard_map.46.white_ref), custom_call_target="tpu_custom_call" | custom-call | tf_op jit(solution)/shard_map/pallas_call | solution.py:167
  23.5 2.3 %shard_map.49 = (f32[544,256]{1,0:T(8,128)S(1)}, bf16[544,256]{1,0:T(8,128)(2,1)}) custom-call(bf16[1024,128]{1,0:T(8,128)(2,1)S(1)} %collective-permute-done.3.theirs_ref, bf16[544,2304]{1,0:T(8,128)(2,1)S(1)} %get-tuple-element.19.keep_ref, bf16[544,2304]{1,0:T(8,128)(2,1)S(1)} %get-tuple-element.20.send_ref), custom_call_target="tpu_custom_call" | custom-call | tf_op jit(solution)/shard_map/pallas_call | solution.py:176
  25.8 0.8 %copy-done.2 = f32[544,256]{1,0:T(8,128)} copy-done((f32[544,256]{1,0:T(8,128)}, f32[544,256]{1,0:T(8,128)S(1)}, u32[]{:S(2)}) %copy-start.2) | copy-done | bytes 557080
  26.6 1.6 %collective-permute-start.4 = (bf16[17,32,256]{2,1,0:T(8,128)(2,1)}, bf16[17,32,256]{2,1,0:T(8,128)(2,1)}, u32[]{:S(2)}, u32[]{:S(2)}) collective-permute-start(bf16[17,32,256]{2,1,0:T(8,128)(2,1)} %bitcast.10), channel_id=1, source_target_pairs={{0,1},{1,0},{2,3},{3,2},{4,5},{5,4},{6,7},{7,6},{8,9},{9,8},{10,11... | collective-permute-start | bytes 835592 | tf_op jit(solution)/shard_map/ppermute | solution.py:130
  28.2 0.7 %compare_reduce_fusion.2 = (pred[]{:T(512)}, s32[]{:T(128)}) fusion(s32[3]{0:T(128)S(1)} %copy-done.7), kind=kLoop, calls=%fused_computation.10 | loop fusion | flops 17 | bytes 17 | tf_op jit(solution)/shard_map/local/reduce | solution.py:164
  28.8 1.7 %copy-done.1 = bf16[544,2304]{1,0:T(8,128)(2,1)S(1)} copy-done((bf16[544,2304]{1,0:T(8,128)(2,1)S(1)}, bf16[544,2304]{1,0:T(8,128)(2,1)}, u32[]{:S(2)}) %copy-start.1) | copy-done | bytes 2506776
  30.6 1.6 %shard_map.48 = (f32[544,256]{1,0:T(8,128)S(1)}, bf16[544,256]{1,0:T(8,128)(2,1)S(1)}) custom-call(bf16[1024,128]{1,0:T(8,128)(2,1)S(1)} %collective-permute-done.theirs_ref, bf16[544,2304]{1,0:T(8,128)(2,1)S(1)} %get-tuple-element.19.keep_ref, bf16[544,2304]{1,0:T(8,128)(2,1)S(1)} %copy-done.1), custom_call_target="tpu_custom_call" | custom-call | tf_op jit(solution)/shard_map/pallas_call | solution.py:176
  32.1 0.5 collective-permute-start.1
  32.7 1.0 %broadcast_select_fusion.theirs_ref = bf16[1024,128]{1,0:T(8,128)(2,1)S(1)} fusion(bf16[1024,128]{1,0:T(8,128)(2,1)S(1)} %select_select_fusion, bf16[1024,128]{1,0:T(8,128)(2,1)} %collective-permute-done.8, pred[]{:T(512)S(6)} %or.8), kind=kLoop, calls=%fused_computation.7 | loop fusion | flops 131072 | bytes 786433 | tf_op jit(solution)/shard_map/jit(_where)/select_n | solution.py:158
  33.6 1.6 %shard_map.50 = (f32[544,256]{1,0:T(8,128)S(1)}, bf16[544,256]{1,0:T(8,128)(2,1)S(1)}) custom-call(bf16[1024,128]{1,0:T(8,128)(2,1)S(1)} %broadcast_select_fusion.theirs_ref, bf16[544,2304]{1,0:T(8,128)(2,1)S(1)} %get-tuple-element.19.keep_ref, bf16[544,2304]{1,0:T(8,128)(2,1)S(1)} %copy-done.1), custom_call_target="tpu_custom_call" | custom-call | tf_op jit(solution)/shard_map/pallas_call | solution.py:176
  35.2 1.6 %collective-permute-start.9 = (bf16[17,32,256]{2,1,0:T(8,128)(2,1)S(1)}, bf16[17,32,256]{2,1,0:T(8,128)(2,1)S(1)}, u32[]{:S(2)}, u32[]{:S(2)}) collective-permute-start(bf16[17,32,256]{2,1,0:T(8,128)(2,1)S(1)} %bitcast.28), channel_id=1, source_target_pairs={{0,1},{1,0},{2,3},{3,2},{4,5},{5,4},{6,7},{7,6},{8,9},{9,8},{10,11... | collective-permute-start | bytes 835592 | tf_op jit(solution)/shard_map/ppermute | solution.py:130
  36.9 1.0 %convert_add_fusion.1 = f32[17,32,256]{2,1,0:T(8,128)S(1)} fusion(f32[17,32,256]{2,1,0:T(8,128)S(1)} %bitcast.20, bf16[17,32,256]{2,1,0:T(8,128)(2,1)} %collective-permute-done.4), kind=kLoop, calls=%fused_computation.1 | loop fusion | flops 278528 | bytes 1392640 | tf_op jit(solution)/shard_map/add | solution.py:198
  38.0 2.7 %collective-permute-start.5 = (bf16[17,16,256]{2,1,0:T(8,128)(2,1)S(1)}, bf16[17,16,256]{2,1,0:T(8,128)(2,1)S(1)}, u32[]{:S(2)}, u32[]{:S(2)}) collective-permute-start(bf16[17,16,256]{2,1,0:T(8,128)(2,1)S(1)} %slice.49), channel_id=1, source_target_pairs={{0,2},{1,3},{2,0},{3,1},{4,6},{5,7},{6,4},{7,5},{8,10},{9,11},{10,... | collective-permute-start | bytes 417800 | tf_op jit(solution)/shard_map/ppermute | solution.py:130
  40.6 4.6 %collective-permute-done.1 = bf16[17,32,256]{2,1,0:T(8,128)(2,1)S(1)} collective-permute-done((bf16[17,32,256]{2,1,0:T(8,128)(2,1)S(1)}, bf16[17,32,256]{2,1,0:T(8,128)(2,1)S(1)}, u32[]{:S(2)}, u32[]{:S(2)}) %collective-permute-start.1) | collective-permute-done | bytes 278560 | tf_op jit(solution)/shard_map/ppermute | solution.py:130
  45.3 1.8 %collective-permute-start.2 = (bf16[17,16,256]{2,1,0:T(8,128)(2,1)S(1)}, bf16[17,16,256]{2,1,0:T(8,128)(2,1)S(1)}, u32[]{:S(2)}, u32[]{:S(2)}) collective-permute-start(bf16[17,16,256]{2,1,0:T(8,128)(2,1)S(1)} %slice.50), channel_id=1, source_target_pairs={{0,2},{1,3},{2,0},{3,1},{4,6},{5,7},{6,4},{7,5},{8,10},{9,11},{10,... | collective-permute-start | bytes 417800 | tf_op jit(solution)/shard_map/ppermute | solution.py:130
  47.1 5.4 %collective-permute-done.9 = bf16[17,32,256]{2,1,0:T(8,128)(2,1)S(1)} collective-permute-done((bf16[17,32,256]{2,1,0:T(8,128)(2,1)S(1)}, bf16[17,32,256]{2,1,0:T(8,128)(2,1)S(1)}, u32[]{:S(2)}, u32[]{:S(2)}) %collective-permute-start.9) | collective-permute-done | bytes 278560 | tf_op jit(solution)/shard_map/ppermute | solution.py:130
  52.7 0.7 %compare_reduce_fusion.1 = (pred[]{:T(512)}, s32[]{:T(128)}) fusion(s32[3]{0:T(128)S(1)} %copy-done.8), kind=kLoop, calls=%fused_computation.9 | loop fusion | flops 17 | bytes 17 | tf_op jit(solution)/shard_map/local/reduce | solution.py:164
  53.4 1.9 %pad_add_fusion.order_ref = s32[3]{0:T(128)S(1)} fusion(s32[1]{0:T(128)} %bitcast.3, s32[1]{0:T(128)} %bitcast.1, s32[1]{0:T(128)} %bitcast), kind=kLoop, calls=%fused_computation.11 | loop fusion | flops 6 | bytes 24 | tf_op jit(solution)/shard_map/stack | solution.py:164
  55.4 5.9 %collective-permute-done.2 = bf16[17,16,256]{2,1,0:T(8,128)(2,1)S(1)} collective-permute-done((bf16[17,16,256]{2,1,0:T(8,128)(2,1)S(1)}, bf16[17,16,256]{2,1,0:T(8,128)(2,1)S(1)}, u32[]{:S(2)}, u32[]{:S(2)}) %collective-permute-start.2) | collective-permute-done | bytes 139296 | tf_op jit(solution)/shard_map/ppermute | solution.py:130
  61.2 1.8 %collective-permute-done.10 = bf16[17,16,256]{2,1,0:T(8,128)(2,1)S(1)} collective-permute-done((bf16[17,16,256]{2,1,0:T(8,128)(2,1)S(1)}, bf16[17,16,256]{2,1,0:T(8,128)(2,1)S(1)}, u32[]{:S(2)}, u32[]{:S(2)}) %collective-permute-start.10) | collective-permute-done | bytes 139296 | tf_op jit(solution)/shard_map/ppermute | solution.py:130
  63.0 1.9 %shard_map.51 = f32[3,65,1024]{2,1,0:T(8,128)} custom-call(s32[3]{0:T(128)S(1)} %pad_add_fusion.order_ref, f32[272,256]{1,0:T(8,128)S(1)} %bitcast.18, bf16[272,256]{1,0:T(8,128)(2,1)S(1)} %bitcast.24, f32[272,256]{1,0:T(8,128)S(1)} %bitcast.17, bf16[272,256]{1,0:T(8,128)(2,1)S(1)} %bitcast.23, f32[272,256]{1,0:T(8,128)S(1)} %bitcast.19, ...), custom_call_target="tpu_custom_call" | custom-call | tf_op jit(solution)/shard_map/pallas_call | solution.py:207
  (30 shorter events, 0.6 us)
Async XLA Ops:
  0.0 1.0 %copy-start.4 = (bf16[1,64,4096]{2,1,0:T(8,128)(2,1)S(1)}, bf16[1,64,4096]{2,1,0:T(8,128)(2,1)}, u32[]{:S(2)}) copy-start(bf16[1,64,4096]{2,1,0:T(8,128)(2,1)} %rec_ref.1) | copy-start | bytes 1572868
  1.0 0.7 %copy-start.5 = (s32[1,2]{1,0:T(1,128)S(1)}, s32[1,2]{1,0:T(1,128)}, u32[]{:S(2)}) copy-start(s32[1,2]{1,0:T(1,128)} %off_ref.1) | copy-start | bytes 28
  1.7 0.7 %copy-start.6 = (bf16[64]{0:T(256)(128)(2,1)S(1)}, bf16[64]{0:T(256)(128)(2,1)}, u32[]{:S(2)}) copy-start(bf16[64]{0:T(256)(128)(2,1)} %param.5) | copy-start | bytes 388
  3.8 10.1 %collective-permute-start.3 = (bf16[1024,128]{1,0:T(8,128)(2,1)S(1)}, bf16[1024,128]{1,0:T(8,128)(2,1)S(1)}, u32[]{:S(2)}, u32[]{:S(2)}) collective-permute-start(bf16[1024,128]{1,0:T(8,128)(2,1)S(1)} %shard_map.46.white_ref), channel_id=1, source_target_pairs={{0,28},{4,24},{8,20},{12,16},{16,12},{20,8},{24,4},{28,0},{1,29},{... | collective-permute-start | bytes 786440 | tf_op jit(solution)/shard_map/ppermute | solution.py:130
  7.2 13.3 %collective-permute-start.6 = (bf16[1024,128]{1,0:T(8,128)(2,1)S(1)}, bf16[1024,128]{1,0:T(8,128)(2,1)S(1)}, u32[]{:S(2)}, u32[]{:S(2)}) collective-permute-start(bf16[1024,128]{1,0:T(8,128)(2,1)S(1)} %shard_map.46.white_ref), channel_id=1, source_target_pairs={{0,8},{4,12},{8,0},{12,4},{16,24},{20,28},{24,16},{28,20},{1,9},{5... | collective-permute-start | bytes 786440 | tf_op jit(solution)/shard_map/ppermute | solution.py:130
  7.7 12.8 %collective-permute-start.7 = (bf16[1024,128]{1,0:T(8,128)(2,1)S(1)}, bf16[1024,128]{1,0:T(8,128)(2,1)S(1)}, u32[]{:S(2)}, u32[]{:S(2)}) collective-permute-start(bf16[1024,128]{1,0:T(8,128)(2,1)S(1)} %shard_map.46.white_ref), channel_id=1, source_target_pairs={{0,16},{4,20},{8,24},{12,28},{16,0},{20,4},{24,8},{28,12},{1,17},{... | collective-permute-start | bytes 786440 | tf_op jit(solution)/shard_map/ppermute | solution.py:130
  8.4 20.4 %collective-permute-start = (bf16[1024,128]{1,0:T(8,128)(2,1)S(1)}, bf16[1024,128]{1,0:T(8,128)(2,1)S(1)}, u32[]{:S(2)}, u32[]{:S(2)}) collective-permute-start(bf16[1024,128]{1,0:T(8,128)(2,1)S(1)} %shard_map.46.white_ref), channel_id=1, source_target_pairs={{0,4},{4,0},{8,12},{12,8},{16,20},{20,16},{24,28},{28,24},{1,5},{5... | collective-permute-start | bytes 786440 | tf_op jit(solution)/shard_map/ppermute | solution.py:130
  20.6 12.1 %collective-permute-start.8 = (bf16[1024,128]{1,0:T(8,128)(2,1)S(1)}, bf16[1024,128]{1,0:T(8,128)(2,1)}, u32[]{:S(2)}, u32[]{:S(2)}) collective-permute-start(bf16[1024,128]{1,0:T(8,128)(2,1)S(1)} %select_select_fusion), channel_id=1, source_target_pairs={{0,4},{4,0},{8,12},{12,8},{16,20},{20,16},{24,28},{28,24},{1,5},{5... | collective-permute-start | bytes 786440 | tf_op jit(solution)/shard_map/ppermute | solution.py:130
  23.5 2.3 %copy-start = (bf16[544,2304]{1,0:T(8,128)(2,1)}, bf16[544,2304]{1,0:T(8,128)(2,1)S(1)}, u32[]{:S(2)}) copy-start(bf16[544,2304]{1,0:T(8,128)(2,1)S(1)} %get-tuple-element.20.send_ref) | copy-start | bytes 7520260
  23.5 4.7 %copy-start.7 = (s32[3]{0:T(128)S(1)}, s32[3]{0:T(128)}, u32[]{:S(2)}) copy-start(s32[3]{0:T(128)} %param.7) | copy-start | bytes 40
  25.8 0.8 %copy-start.2 = (f32[544,256]{1,0:T(8,128)}, f32[544,256]{1,0:T(8,128)S(1)}, u32[]{:S(2)}) copy-start(f32[544,256]{1,0:T(8,128)S(1)} %get-tuple-element.23) | copy-start | bytes 1671172
  26.6 10.3 %collective-permute-start.4 = (bf16[17,32,256]{2,1,0:T(8,128)(2,1)}, bf16[17,32,256]{2,1,0:T(8,128)(2,1)}, u32[]{:S(2)}, u32[]{:S(2)}) collective-permute-start(bf16[17,32,256]{2,1,0:T(8,128)(2,1)} %bitcast.10), channel_id=1, source_target_pairs={{0,1},{1,0},{2,3},{3,2},{4,5},{5,4},{6,7},{7,6},{8,9},{9,8},{10,11... | collective-permute-start | bytes 835592 | tf_op jit(solution)/shard_map/ppermute | solution.py:130
  28.8 1.7 %copy-start.1 = (bf16[544,2304]{1,0:T(8,128)(2,1)S(1)}, bf16[544,2304]{1,0:T(8,128)(2,1)}, u32[]{:S(2)}) copy-start(bf16[544,2304]{1,0:T(8,128)(2,1)} %copy-done) | copy-start | bytes 7520260
  32.1 13.1 %collective-permute-start.1 = (bf16[17,32,256]{2,1,0:T(8,128)(2,1)S(1)}, bf16[17,32,256]{2,1,0:T(8,128)(2,1)S(1)}, u32[]{:S(2)}, u32[]{:S(2)}) collective-permute-start(bf16[17,32,256]{2,1,0:T(8,128)(2,1)S(1)} %bitcast.27), channel_id=1, source_target_pairs={{0,1},{1,0},{2,3},{3,2},{4,5},{5,4},{6,7},{7,6},{8,9},{9,8},{10,11... | collective-permute-start | bytes 835592 | tf_op jit(solution)/shard_map/ppermute | solution.py:130
  33.6 3.2 %copy-start.3 = (f32[544,256]{1,0:T(8,128)S(1)}, f32[544,256]{1,0:T(8,128)}, u32[]{:S(2)}) copy-start(f32[544,256]{1,0:T(8,128)} %copy-done.2) | copy-start | bytes 1671172
  35.2 17.2 %collective-permute-start.9 = (bf16[17,32,256]{2,1,0:T(8,128)(2,1)S(1)}, bf16[17,32,256]{2,1,0:T(8,128)(2,1)S(1)}, u32[]{:S(2)}, u32[]{:S(2)}) collective-permute-start(bf16[17,32,256]{2,1,0:T(8,128)(2,1)S(1)} %bitcast.28), channel_id=1, source_target_pairs={{0,1},{1,0},{2,3},{3,2},{4,5},{5,4},{6,7},{7,6},{8,9},{9,8},{10,11... | collective-permute-start | bytes 835592 | tf_op jit(solution)/shard_map/ppermute | solution.py:130
  36.9 15.8 %copy-start.8 = (s32[3]{0:T(128)S(1)}, s32[3]{0:T(128)}, u32[]{:S(2)}) copy-start(s32[3]{0:T(128)} %param.7) | copy-start | bytes 40
  38.0 17.4 %collective-permute-start.5 = (bf16[17,16,256]{2,1,0:T(8,128)(2,1)S(1)}, bf16[17,16,256]{2,1,0:T(8,128)(2,1)S(1)}, u32[]{:S(2)}, u32[]{:S(2)}) collective-permute-start(bf16[17,16,256]{2,1,0:T(8,128)(2,1)S(1)} %slice.49), channel_id=1, source_target_pairs={{0,2},{1,3},{2,0},{3,1},{4,6},{5,7},{6,4},{7,5},{8,10},{9,11},{10,... | collective-permute-start | bytes 417800 | tf_op jit(solution)/shard_map/ppermute | solution.py:130
  45.3 15.9 %collective-permute-start.2 = (bf16[17,16,256]{2,1,0:T(8,128)(2,1)S(1)}, bf16[17,16,256]{2,1,0:T(8,128)(2,1)S(1)}, u32[]{:S(2)}, u32[]{:S(2)}) collective-permute-start(bf16[17,16,256]{2,1,0:T(8,128)(2,1)S(1)} %slice.50), channel_id=1, source_target_pairs={{0,2},{1,3},{2,0},{3,1},{4,6},{5,7},{6,4},{7,5},{8,10},{9,11},{10,... | collective-permute-start | bytes 417800 | tf_op jit(solution)/shard_map/ppermute | solution.py:130
  52.6 10.4 %collective-permute-start.10 = (bf16[17,16,256]{2,1,0:T(8,128)(2,1)S(1)}, bf16[17,16,256]{2,1,0:T(8,128)(2,1)S(1)}, u32[]{:S(2)}, u32[]{:S(2)}) collective-permute-start(bf16[17,16,256]{2,1,0:T(8,128)(2,1)S(1)} %slice.48), channel_id=1, source_target_pairs={{0,2},{1,3},{2,0},{3,1},{4,6},{5,7},{6,4},{7,5},{8,10},{9,11},{10,... | collective-permute-start | bytes 417800 | tf_op jit(solution)/shard_map/ppermute | solution.py:130
where the time goes:
time: 65.3 us; the launch traced here: 64.9 us
  waiting for transfers between devices  26.4 us (40%)
  starting transfers between devices  13 us (20%)
  Pallas kernels  10.2 us (16%)
  other arithmetic  6.78 us (10%)
  local copies, waits for them, and re-layouts  6.43 us (10%)
  between operations  2.07 us (3%)
    ppermute x11, waiting for transfers between devices, apart(): lax.ppermute(value, axis, [(s, s ^ mask) for s in range(lax.axis_size(axi...  26.4 us
    ppermute x11, starting transfers between devices, apart(): lax.ppermute(value, axis, [(s, s ^ mask) for s in range(lax.axis_size(axi...  13 us
    pallas_call x3, Pallas kernels, correlate(): pl.pallas_call(correlate_kernel, out_shape=[jax.ShapeDtypeStruct((half_ro...  5.43 us
    unnamed x18, local copies, waits for them, and re-layouts  4.88 us
    another operation x3, other arithmetic, local(): jnp.argmax(pair_masks == m).astype(jnp.int32)  2.69 us
    pallas_call x1, Pallas kernels, local(): pl.pallas_call(functools.partial(finish_kernel, share, norm), out_shape=j...  1.92 us
    another operation x1, other arithmetic, local(): jnp.stack([jnp.argmax(pair_masks == m).astype(jnp.int32) for m in (jnp.in...  1.89 us
    pallas_call x1, Pallas kernels, local(): pl.pallas_call(whiten_kernel, out_shape=jax.ShapeDtypeStruct((L, 2 * chan...  1.43 us
  transfers between devices with their start and end apart: 11, of which 6 were waited for; matrix products, arithmetic and copies ran while one was open for 13% of the time, Pallas kernels for 11%

commit v1 on v0

v1 whole, which is shorter than its diff:
```python
import functools

import jax
import jax.numpy as jnp
from jax import lax
from jax.experimental import pallas as pl
from jax.experimental.pallas import tpu as pltpu
from jax.sharding import PartitionSpec as P

L = 1024
MAXLAG = 32
LAGS = 2 * MAXLAG + 1
FINE = 16
COARSE = 4
PLANES = FINE + 1
PAD = 1152
CUT = 1280
COST = 1.0
DIRECT_ORDER = (2, 3, 1)
FAR_AFTER = False
LAST_AFTER = 1
LATE_Z = False
NEAR_FIRST = False
FAR, FREE = "low", "low"
NT = (((1,), (1,)), ((), ()))
VMEM = pl.BlockSpec(memory_space=pltpu.VMEM)
SMEM = pl.BlockSpec(memory_space=pltpu.SMEM)
HBM = pl.BlockSpec(memory_space=pltpu.HBM)


def call(kernel, out_shape, in_specs, scratch=(), micros=1.0, vmem=24):
    many = isinstance(out_shape, list)
    return pl.pallas_call(
        kernel,
        out_shape=out_shape,
        in_specs=in_specs,
        out_specs=[VMEM] * len(out_shape) if many else VMEM,
        scratch_shapes=list(scratch),
        compiler_params=pltpu.CompilerParams(vmem_limit_bytes=vmem * 1024 * 1024),
        cost_estimate=pl.CostEstimate(flops=int(micros * COST * 1e9), bytes_accessed=int(micros * COST * 3e6), transcendentals=0),
    )


def whiten_kernel(off_hbm, taps_hbm, rec_hbm, out_ref, off_ref, taps_ref, rec_ref, wide_ref, sems):
    copies = [
        pltpu.make_async_copy(src, dst, sems.at[k])
        for k, (src, dst) in enumerate(((off_hbm, off_ref), (rec_hbm, rec_ref), (taps_hbm, taps_ref)))
    ]
    for copy in copies:
        copy.start()
    chans, rec_len = rec_ref.shape[1], rec_ref.shape[2]
    wide_ref[...] = jnp.zeros_like(wide_ref)
    copies[2].wait()
    copies[0].wait()
    taps = taps_ref[...].astype(jnp.float32)
    row = jnp.concatenate([taps, jnp.zeros((1, 384 - taps.shape[1]), jnp.float32)], axis=1)
    row = jnp.broadcast_to(row, (8, 384))
    bands, bases = [], []
    for w in range(2):
        start = off_ref[0, w]
        base = jnp.minimum((start // 128) * 128, rec_len - CUT)
        bases.append(pl.multiple_of(base, 128))
        moved = pltpu.roll(row, start - base, 1)
        block = jnp.broadcast_to(moved[0:1], (128, 384))
        block = pltpu.roll(block, 0, 1, stride=1, stride_axis=0).astype(jnp.bfloat16)
        none = jnp.zeros((128, 128), jnp.bfloat16)
        bands.append(
            jnp.concatenate(
                [jnp.concatenate([block, none], axis=1), jnp.concatenate([none, block], axis=1)],
                axis=0,
            )
        )
    copies[1].wait()
    for w in range(2):
        wide_ref[w, w * chans : (w + 1) * chans, :] = rec_ref[0, :, pl.ds(bases[w], CUT)]
    parts = []
    for c in range(L // 256):
        part = lax.dot_general(
            bands[0], wide_ref[0, :, c * 256 : c * 256 + 512], NT, preferred_element_type=jnp.float32
        )
        part += lax.dot_general(
            bands[1], wide_ref[1, :, c * 256 : c * 256 + 512], NT, preferred_element_type=jnp.float32
        )
        parts.append(part)
    power = sum(jnp.sum(part * part, axis=0, keepdims=True) for part in parts) * (1.0 / L)
    scale = lax.rsqrt(power + 1e-06)
    for c, part in enumerate(parts):
        out_ref[c * 256 : (c + 1) * 256, :] = (part * scale).astype(jnp.bfloat16)


def prepare_kernel(days, count, white_ref, lhs_ref):
    chans = white_ref.shape[1] // 2
    share = chans // days
    bits = days.bit_length() - 1
    me = lax.axis_index("day")
    rows = lax.broadcasted_iota(jnp.int32, (2 * chans, 2 * chans), 0)
    cols = lax.broadcasted_iota(jnp.int32, (2 * chans, 2 * chans), 1)
    place = (rows % chans) // share
    slot = jnp.zeros_like(place)
    for b in range(bits):
        slot = slot + (((place >> b) & 1) << (bits - 1 - b))
    source = (rows // chans) * chans + (slot ^ me) * share + rows % share
    pick = (cols == source).astype(jnp.float32).astype(jnp.bfloat16)
    mine = lax.dot_general(pick, white_ref[...], NT, preferred_element_type=jnp.float32)
    mine = jnp.concatenate([mine, jnp.zeros((2 * chans, PAD - L), jnp.float32)], axis=1)
    for p in range(PLANES):
        moved = (pltpu.roll(mine, p, 1) if p else mine).astype(jnp.bfloat16)
        for w in range(2):
            for b in range(count):
                at = (b * PLANES + p) * share
                lhs_ref[at : at + share, w * PAD : (w + 1) * PAD] = moved[w * chans + b * share : w * chans + (b + 1) * share]


def fill_weights(theirs, w_ref):
    theirs = theirs.astype(jnp.float32)
    swapped = pltpu.roll(theirs, 64, 1)
    low = lax.broadcasted_iota(jnp.int32, (1, 128), 1) < 64
    zero = jnp.zeros((16, 128), jnp.float32)
    for w, (a, b) in enumerate(((theirs, swapped), (swapped, theirs))):
        first = jnp.concatenate([zero, zero, a, zero, zero, zero, zero], axis=0)
        second = jnp.concatenate([zero, b, zero, zero, zero, zero, zero], axis=0)
        both = jnp.where(low, first, second).astype(jnp.bfloat16)
        rows = both.shape[0]
        w_ref[w * PAD : w * PAD + rows, 0:128] = both
        w_ref[w * PAD + rows : (w + 1) * PAD, 0:128] = jnp.zeros((PAD - rows, 128), jnp.bfloat16)
        w_ref[w * PAD : w * PAD + rows - 32, 128:256] = both[32:]
        w_ref[w * PAD + rows - 32 : (w + 1) * PAD, 128:256] = jnp.zeros((PAD - rows + 32, 128), jnp.bfloat16)


def correlate(places, theirs, lhs_ref, out_refs, w_ref):
    fill_weights(theirs, w_ref)
    weights = w_ref[...]
    half = lhs_ref.shape[0] // 2
    size = lhs_ref.shape[0] // len(places)
    for base in (half, 0):
        part = jnp.dot(lhs_ref[base : base + half, :], weights, preferred_element_type=jnp.float32)
        for place, (index, at) in enumerate(places):
            row = place * size - base
            if 0 <= row < half:
                ref = out_refs[index]
                ref[at * size : (at + 1) * size, :] = part[row : row + size].astype(ref.dtype)


def paired_kernel(theirs_ref, lhs_ref, theirs2_ref, lhs2_ref, kept_ref, sent_ref, w_ref, sum_ref):
    half = lhs2_ref.shape[0]
    fill_weights(theirs_ref[...], w_ref)
    sum_ref[...] = jnp.dot(lhs_ref[0:half, :], w_ref[...], preferred_element_type=jnp.float32)
    fill_weights(theirs2_ref[...], w_ref)
    total = sum_ref[...] + jnp.dot(lhs2_ref[...], w_ref[...], preferred_element_type=jnp.float32)
    size = kept_ref.shape[0]
    kept_ref[...] = total[0:size]
    sent_ref[...] = total[size:].astype(jnp.bfloat16)


def known_kernel(places, theirs_ref, lhs_ref, *refs):
    correlate(places, theirs_ref[...], lhs_ref, refs[:-1], refs[-1])


def third_mask(masks_ref, last):
    return masks_ref[0] ^ masks_ref[1] ^ masks_ref[2] ^ 1 ^ last


def other_core(third):
    return (third == 3) | (third == 5)


def passed_kernel(last, masks_ref, white_ref, near_ref, out_ref):
    flip = other_core(third_mask(masks_ref, last))

    @pl.when(flip)
    def _():
        out_ref[...] = near_ref[...]

    @pl.when(jnp.logical_not(flip))
    def _():
        out_ref[...] = white_ref[...]


def chosen_kernel(places, last, masks_ref, x_ref, y_ref, corner_ref, lhs_ref, *refs):
    outs, w_ref, theirs_ref = refs[:-2], refs[-2], refs[-1]
    chip = third_mask(masks_ref, last) >> 1
    for k, ref in enumerate((x_ref, y_ref, corner_ref)):

        @pl.when(chip == k + 1)
        def _(ref=ref):
            theirs_ref[...] = ref[...]

    correlate(places, theirs_ref[...], lhs_ref, outs, w_ref)


def finish_kernel(share, norm, last, counts, masks_ref, *refs):
    ins, out_ref, s_ref = list(refs[:-2]), refs[-2], refs[-1]
    low = lax.broadcasted_iota(jnp.int32, (1, 128), 1) < 64
    third = third_mask(masks_ref, last)
    rows = PLANES * share
    for k, mask in enumerate((1, last, third)):
        total = sum(ins.pop(0)[0:rows, :].astype(jnp.float32) for _ in range(counts[k])) * norm
        s_ref[0] = total[:, 0:128]
        s_ref[1] = total[:, 128:256]
        r = jnp.where(masks_ref[0] == mask, 0, jnp.where(masks_ref[1] == mask, 1, 2))
        for pair in range(share // 2):
            to = slice(pair * 128, pair * 128 + 128)
            for tile in range(COARSE // 2):
                one = s_ref[tile, pl.ds(2 * pair, FINE, stride=share), :]
                two = s_ref[tile, pl.ds(2 * pair + 1, FINE, stride=share), :]
                q = 2 * tile * FINE
                out_ref[r, q : q + FINE, to] = jnp.where(low, one, pltpu.roll(two, 64, 1))
                out_ref[r, q + FINE : q + 2 * FINE, to] = jnp.where(low, pltpu.roll(one, 64, 1), two)
            one = s_ref[1, FINE * share + 2 * pair : FINE * share + 2 * pair + 1, :]
            two = s_ref[1, FINE * share + 2 * pair + 1 : FINE * share + 2 * pair + 2, :]
            out_ref[r, LAGS - 1 : LAGS, to] = jnp.where(low, pltpu.roll(one, 64, 1), two)


def apart(value, axis, mask):
    return lax.ppermute(value, axis, [(s, s ^ mask) for s in range(lax.axis_size(axis))])


def local(records, filter_taps, window_offsets, pair_masks):
    chans, rec_len = records.shape[1], records.shape[2]
    taps = filter_taps.shape[0]
    blocks = lax.axis_size("chan")
    days = lax.axis_size("day")
    share = chans // days
    last = blocks - 1
    bf16, f32 = jnp.bfloat16, jnp.float32
    white = call(
        whiten_kernel,
        jax.ShapeDtypeStruct((L, 2 * chans), bf16),
        [HBM] * 3,
        [
            pltpu.SMEM((1, 2), jnp.int32),
            pltpu.VMEM((1, taps), bf16),
            pltpu.VMEM((1, chans, rec_len), bf16),
            pltpu.VMEM((2, 2 * chans, CUT), bf16),
            pltpu.SemaphoreType.DMA((3,)),
        ],
        micros=2.0,
        vmem=63,
    )(window_offsets, filter_taps.reshape(1, -1), records)

    near = apart(white, "chan", 1)
    far = apart(white, "chan", last)
    if days == 4:
        white2 = apart(lax.optimization_barrier((white, near))[0] if LATE_Z else white, "day", 1)

    def prepare(block, count):
        return call(
            functools.partial(prepare_kernel, days, count),
            jax.ShapeDtypeStruct((PLANES * share * count, 2 * PAD), bf16),
            [VMEM],
            micros=1.5,
        )(block)

    lhs = prepare(white, days)

    slot_rows = PLANES * share
    weights = pltpu.VMEM((2 * PAD, 256), bf16)

    def reverse(slot):
        return sum(((slot >> b) & 1) << (days.bit_length() - 2 - b) for b in range(days.bit_length() - 1))

    def plan(mode):
        if mode == "direct":
            return list(DIRECT_ORDER), [([slot], bf16 if slot else f32) for slot in range(days)]
        steps = [1 << b for b in range(days.bit_length() - 1)]
        if mode == "high":
            steps = steps[::-1]
        left, outs = list(range(days)), []
        for step in steps:
            outs.insert(0, ([slot for slot in left if slot & step], bf16 if len(left) == days else f32))
            left = [slot for slot in left if not slot & step]
        return steps, [(left, f32)] + outs

    def started(mode, steps, outs, parts):
        if mode == "direct":
            came = [parts[0]] + [apart(parts[s], "day", s) for s in steps]
            return lambda after=None: came
        kept = list(parts[:-1])
        came = [apart(parts[-1], "day", steps[0])]
        held = [[slot ^ steps[0] for slot in outs[-1][0]]]

        def rest(after=None):
            if after is not None:
                came[0], _ = lax.optimization_barrier((came[0], after))
            for step in steps[1:]:
                piece, slots = kept.pop(), outs[len(kept)][0]
                n = piece.shape[0]
                for c, slots_c in zip(came, held):
                    at = slots_c.index(slots[0]) * slot_rows
                    piece = piece + c[at : at + n].astype(f32)
                held.append([slot ^ step for slot in slots])
                came.append(apart(piece.astype(bf16), "day", step))
            return [kept[0]] + came

        rest.came = came
        return rest

    def day_sum(mode, theirs, pick=None):
        mode = mode if days == 4 else "low"
        steps, outs = plan(mode)
        shapes = [jax.ShapeDtypeStruct((len(slots) * slot_rows, 256), kind) for slots, kind in outs]
        where = {slot: (k, at) for k, (slots, _) in enumerate(outs) for at, slot in enumerate(slots)}
        places = [where[reverse(place)] for place in range(days)]
        if pick is None:
            parts = call(functools.partial(known_kernel, places), shapes, [VMEM] * 2, [weights], micros=2.0)(theirs, lhs)
        else:
            parts = call(
                functools.partial(chosen_kernel, places, last),
                shapes,
                [SMEM] + [VMEM] * (len(theirs) + 1),
                [weights, pltpu.VMEM((L, 2 * chans), bf16)],
                micros=2.0,
            )(pick, *theirs, lhs)
        return parts[-1], started(mode, steps, outs, parts)

    if blocks == 8:
        passed = call(
            functools.partial(passed_kernel, last),
            jax.ShapeDtypeStruct(white.shape, bf16),
            [SMEM] + [VMEM] * 2,
            micros=0.5,
        )(pair_masks, white, near)
        along_x = apart(passed, "chan", 2)
        along_y = apart(passed, "chan", 4)
    far_done, far_sum = day_sum(FAR, far)
    if days == 4:
        white2, _ = lax.optimization_barrier((white2, far_done))
        near2 = apart(white2, "chan", 1)
        near_kept, near_done = call(
            paired_kernel,
            [jax.ShapeDtypeStruct((slot_rows, 256), f32), jax.ShapeDtypeStruct((slot_rows, 256), bf16)],
            [VMEM] * 4,
            [weights, pltpu.VMEM((2 * slot_rows, 256), f32)],
            micros=2.0,
        )(near, lhs, near2, prepare(white2, 2))
        near_came = [near_kept, apart(near_done, "day", 2)]
    else:
        near_done, near_sum = day_sum("low", near)
        near_came = near_sum()
    if blocks == 8:
        corner = apart(far, "chan", 1)
        if NEAR_FIRST:
            along_x, along_y, _ = lax.optimization_barrier((along_x, along_y, near_done))
        free_done, free_sum = day_sum(FREE, (along_x, along_y, corner), pair_masks)
    else:
        free = white
        third = pair_masks[0] ^ pair_masks[1] ^ pair_masks[2] ^ 1 ^ last
        for bit in range(blocks.bit_length() - 1):
            free = jnp.where(((third >> bit) & 1) == 1, apart(free, "chan", 2**bit), free)
        free_done, free_sum = day_sum(FREE, free)
    far_came = far_sum(free_done if FAR_AFTER else None)
    sums = [near_came, far_came, free_sum((None, near_came[-1], (near_came[-1], far_came[-1]))[LAST_AFTER])]

    day_total = records.shape[0] * days
    norm = float((day_total * window_offsets.shape[1] * L) ** -0.5)
    flat = [part for group in sums for part in group]
    return call(
        functools.partial(finish_kernel, share, norm, last, [len(group) for group in sums]),
        jax.ShapeDtypeStruct((3, LAGS, share * chans), f32),
        [SMEM] + [VMEM] * len(flat),
        [pltpu.VMEM((2, slot_rows, 128), f32)],
        micros=2.0,
    )(pair_masks, *flat)


def solution(mesh):
    in_specs = (P("day", "chan", None), P(), P("day", None), P())
    out_specs = P(None, None, ("chan", "day"))
    return jax.shard_map(local, mesh=mesh, in_specs=in_specs, out_specs=out_specs, check_vma=False)
```

time: 65.3 us -> 47.4 us (0.73)
  the two profiles are of different devices: /device:TPU:0 before, /device:TPU:26 now
where the time goes in v1:
time: 47.4 us; the launch traced here: 47.3 us
  waiting for transfers between devices  24.2 us (51%)
  Pallas kernels  12.7 us (27%)
  starting transfers between devices  9.18 us (19%)
  local copies, waits for them, and re-layouts  0.99 us (2%)
    ppermute x12, waiting for transfers between devices, apart(): lax.ppermute(value, axis, [(s, s ^ mask) for s in range(lax.axis_size(axi...  24.2 us
    ppermute x12, starting transfers between devices, apart(): lax.ppermute(value, axis, [(s, s ^ mask) for s in range(lax.axis_size(axi...  9.18 us
    pallas_call x1, Pallas kernels, local(): call(whiten_kernel, jax.ShapeDtypeStruct((L, 2 * chans), bf16), [HBM] * 3...  2.55 us
    pallas_call x2, Pallas kernels, prepare(): call(functools.partial(prepare_kernel, days, count), jax.ShapeDtypeStruct...  2.24 us
    pallas_call x1, Pallas kernels, day_sum(): call(functools.partial(chosen_kernel, places, last), shapes, [SMEM] + [VM...  2.14 us
    pallas_call x1, Pallas kernels, local(): call(functools.partial(finish_kernel, share, norm, last, [len(group) for...  1.95 us
    pallas_call x1, Pallas kernels, local(): call(paired_kernel, [jax.ShapeDtypeStruct((slot_rows, 256), f32), jax.Sha...  1.69 us
    pallas_call x1, Pallas kernels, day_sum(): call(functools.partial(known_kernel, places), shapes, [VMEM] * 2, [weight...  1.57 us
  transfers between devices with their start and end apart: 12, of which 6 were waited for; matrix products, arithmetic and copies ran while one was open for 0% of the time, Pallas kernels for 17%

profile of v1, /device:TPU:26, one launch (start us, length us, event | category | flops | bytes accessed | tf_op | source)
XLA Modules:
  0.0 47.3 jit_solution(14106348182686888607)
XLA Ops:
  0.0 2.5 %shard_map.46.white_ref = bf16[1024,128]{1,0:T(8,128)(2,1)} custom-call(s32[1,2]{1,0:T(1,128)} %off_hbm.1, bf16[1,64]{1,0:T(2,128)(2,1)} %bitcast.1, bf16[1,64,4096]{2,1,0:T(8,128)(2,1)} %rec_hbm.1), custom_call_target="tpu_custom_call" | custom-call | flops 2000000000 | bytes 6000000 | tf_op jit(solution)/shard_map/pallas_call | solution.py:226
  2.6 0.1 collective-permute-start
  2.6 1.6 %collective-permute-start.2 = (bf16[1024,128]{1,0:T(8,128)(2,1)}, bf16[1024,128]{1,0:T(8,128)(2,1)S(1)}, u32[]{:S(2)}, u32[]{:S(2)}) collective-permute-start(bf16[1024,128]{1,0:T(8,128)(2,1)} %shard_map.46.white_ref), channel_id=1, source_target_pairs={{0,28},{4,24},{8,20},{12,16},{16,12},{20,8},{24,4},{28,0},{1,29},{... | collective-permute-start | bytes 786440 | tf_op jit(solution)/shard_map/ppermute | solution.py:215
  4.2 0.4 collective-permute-start.1
  4.7 1.0 %copy-done = bf16[1024,128]{1,0:T(8,128)(2,1)S(1)} copy-done((bf16[1024,128]{1,0:T(8,128)(2,1)S(1)}, bf16[1024,128]{1,0:T(8,128)(2,1)}, u32[]{:S(2)}) %copy-start) | copy-done | bytes 262168
  5.7 1.4 %shard_map.47.lhs_ref = bf16[1088,2304]{1,0:T(8,128)(2,1)S(1)} custom-call(bf16[1024,128]{1,0:T(8,128)(2,1)S(1)} %copy-done), custom_call_target="tpu_custom_call" | custom-call | flops 1500000000 | bytes 4500000 | tf_op jit(solution)/shard_map/pallas_call | solution.py:247
  7.1 0.0 collective-permute-done.theirs_ref.near_ref
  7.1 0.6 %shard_map.51 = bf16[1024,128]{1,0:T(8,128)(2,1)S(1)} custom-call(s32[3]{0:T(128)S(1)} %copy-done.2, bf16[1024,128]{1,0:T(8,128)(2,1)S(1)} %copy-done.1, bf16[1024,128]{1,0:T(8,128)(2,1)S(1)} %collective-permute-done.theirs_ref.near_ref), custom_call_target="tpu_custom_call" | custom-call | flops 500000000 | bytes 1500000 | tf_op jit(solution)/shard_map/pallas_call | solution.py:317
  7.7 1.6 %collective-permute-start.7 = (bf16[1024,128]{1,0:T(8,128)(2,1)S(1)}, bf16[1024,128]{1,0:T(8,128)(2,1)S(1)}, u32[]{:S(2)}, u32[]{:S(2)}) collective-permute-start(bf16[1024,128]{1,0:T(8,128)(2,1)S(1)} %shard_map.51), channel_id=1, source_target_pairs={{0,8},{4,12},{8,0},{12,4},{16,24},{20,28},{24,16},{28,20},{1,9},{5... | collective-permute-start | bytes 786440 | tf_op jit(solution)/shard_map/ppermute | solution.py:215
  9.3 0.5 %collective-permute-start.8 = (bf16[1024,128]{1,0:T(8,128)(2,1)S(1)}, bf16[1024,128]{1,0:T(8,128)(2,1)S(1)}, u32[]{:S(2)}, u32[]{:S(2)}) collective-permute-start(bf16[1024,128]{1,0:T(8,128)(2,1)S(1)} %shard_map.51), channel_id=1, source_target_pairs={{0,16},{4,20},{8,24},{12,28},{16,0},{20,4},{24,8},{28,12},{1,17},{... | collective-permute-start | bytes 786440 | tf_op jit(solution)/shard_map/ppermute | solution.py:215
  9.8 2.1 %collective-permute-done.2.theirs_ref = bf16[1024,128]{1,0:T(8,128)(2,1)S(1)} collective-permute-done((bf16[1024,128]{1,0:T(8,128)(2,1)}, bf16[1024,128]{1,0:T(8,128)(2,1)S(1)}, u32[]{:S(2)}, u32[]{:S(2)}) %collective-permute-start.2) | collective-permute-done | bytes 262176 | tf_op jit(solution)/shard_map/ppermute | solution.py:215
  11.9 0.9 %collective-permute-start.9 = (bf16[1024,128]{1,0:T(8,128)(2,1)S(1)}, bf16[1024,128]{1,0:T(8,128)(2,1)S(1)}, u32[]{:S(2)}, u32[]{:S(2)}) collective-permute-start(bf16[1024,128]{1,0:T(8,128)(2,1)S(1)} %collective-permute-done.2.theirs_ref), channel_id=1, source_target_pairs={{0,4},{4,0},{8,12},{12,8},{16,20},{20,16},{24,28},{28,24},{1,5},{5... | collective-permute-start | bytes 786440 | tf_op jit(solution)/shard_map/ppermute | solution.py:215
  12.8 1.6 %shard_map.48 = (f32[272,256]{1,0:T(8,128)S(1)}, f32[272,256]{1,0:T(8,128)S(1)}, bf16[544,256]{1,0:T(8,128)(2,1)S(1)}) custom-call(bf16[1024,128]{1,0:T(8,128)(2,1)S(1)} %collective-permute-done.2.theirs_ref, bf16[1088,2304]{1,0:T(8,128)(2,1)S(1)} %shard_map.47.lhs_ref), custom_call_target="tpu_custom_call" | custom-call | flops 2000000000 | bytes 6000000 | tf_op jit(solution)/shard_map/pallas_call | solution.py:305
  14.4 0.5 %collective-permute-start.5 = (bf16[544,256]{1,0:T(8,128)(2,1)S(1)}, bf16[544,256]{1,0:T(8,128)(2,1)S(1)}, u32[]{:S(2)}, u32[]{:S(2)}) collective-permute-start(bf16[544,256]{1,0:T(8,128)(2,1)S(1)} %get-tuple-element.15), channel_id=1, source_target_pairs={{0,1},{1,0},{2,3},{3,2},{4,5},{5,4},{6,7},{7,6},{8,9},{9,8},{10,11... | collective-permute-start | bytes 835592 | tf_op jit(solution)/shard_map/ppermute | solution.py:215
  14.9 0.0 collective-permute-done.1.white_ref
  14.9 0.0 collective-permute-start.3
  14.9 0.8 %shard_map.49.lhs2_ref = bf16[544,2304]{1,0:T(8,128)(2,1)S(1)} custom-call(bf16[1024,128]{1,0:T(8,128)(2,1)S(1)} %collective-permute-done.1.white_ref), custom_call_target="tpu_custom_call" | custom-call | flops 1500000000 | bytes 4500000 | tf_op jit(solution)/shard_map/pallas_call | solution.py:247
  15.7 2.4 %collective-permute-done.7.x_ref = bf16[1024,128]{1,0:T(8,128)(2,1)S(1)} collective-permute-done((bf16[1024,128]{1,0:T(8,128)(2,1)S(1)}, bf16[1024,128]{1,0:T(8,128)(2,1)S(1)}, u32[]{:S(2)}, u32[]{:S(2)}) %collective-permute-start.7) | collective-permute-done | bytes 262176 | tf_op jit(solution)/shard_map/ppermute | solution.py:215
  18.1 0.0 collective-permute-done.8.y_ref
  18.1 0.0 collective-permute-done.9.corner_ref
  18.1 2.1 %shard_map.52 = (f32[272,256]{1,0:T(8,128)S(1)}, f32[272,256]{1,0:T(8,128)S(1)}, bf16[544,256]{1,0:T(8,128)(2,1)S(1)}) custom-call(s32[3]{0:T(128)S(1)} %copy-done.2, bf16[1024,128]{1,0:T(8,128)(2,1)S(1)} %collective-permute-done.7.x_ref, bf16[1024,128]{1,0:T(8,128)(2,1)S(1)} %collective-permute-done.8.y_ref, ...), custom_call_target="tpu_custom_call" | custom-call | flops 2000000000 | bytes 6000000 | tf_op jit(solution)/shard_map/pallas_call | solution.py:307
  20.2 0.8 %collective-permute-start.10 = (bf16[544,256]{1,0:T(8,128)(2,1)S(1)}, bf16[544,256]{1,0:T(8,128)(2,1)S(1)}, u32[]{:S(2)}, u32[]{:S(2)}) collective-permute-start(bf16[544,256]{1,0:T(8,128)(2,1)S(1)} %get-tuple-element.22), channel_id=1, source_target_pairs={{0,1},{1,0},{2,3},{3,2},{4,5},{5,4},{6,7},{7,6},{8,9},{9,8},{10,11... | collective-permute-start | bytes 835592 | tf_op jit(solution)/shard_map/ppermute | solution.py:215
  21.0 0.0 collective-permute-done.3.theirs2_ref
  21.0 1.7 %shard_map.50 = (f32[272,256]{1,0:T(8,128)S(1)}, bf16[272,256]{1,0:T(8,128)(2,1)S(1)}) custom-call(bf16[1024,128]{1,0:T(8,128)(2,1)S(1)} %collective-permute-done.theirs_ref.near_ref, bf16[1088,2304]{1,0:T(8,128)(2,1)S(1)} %shard_map.47.lhs_ref, bf16[1024,128]{1,0:T(8,128)(2,1)S(1)} %collective-permute-done.3.theirs2_ref, ...), custom_call_target="tpu_custom_call" | custom-call | flops 2000000000 | bytes 6000000 | tf_op jit(solution)/shard_map/pallas_call | solution.py:329
  22.7 0.4 collective-permute-start.4
  23.1 0.4 collective-permute-done.5.refs_3_
  23.5 2.3 %collective-permute-start.6 = (bf16[272,256]{1,0:T(8,128)(2,1)S(1)}, bf16[272,256]{1,0:T(8,128)(2,1)S(1)}, u32[]{:S(2)}, u32[]{:S(2)}) collective-permute-start(bf16[272,256]{1,0:T(8,128)(2,1)S(1)} %add_convert_fusion.1), channel_id=1, source_target_pairs={{0,2},{1,3},{2,0},{3,1},{4,6},{5,7},{6,4},{7,5},{8,10},{9,11},{10,... | collective-permute-start | bytes 417800 | tf_op jit(solution)/shard_map/ppermute | solution.py:215
  25.8 13.4 %collective-permute-done.4.refs_1_ = bf16[272,256]{1,0:T(8,128)(2,1)S(1)} collective-permute-done((bf16[272,256]{1,0:T(8,128)(2,1)S(1)}, bf16[272,256]{1,0:T(8,128)(2,1)S(1)}, u32[]{:S(2)}, u32[]{:S(2)}) %collective-permute-start.4) | collective-permute-done | bytes 139296 | tf_op jit(solution)/shard_map/ppermute | solution.py:215
  39.3 0.1 collective-permute-start.11
  39.4 2.4 %collective-permute-done.6.refs_4_ = bf16[272,256]{1,0:T(8,128)(2,1)S(1)} collective-permute-done((bf16[272,256]{1,0:T(8,128)(2,1)S(1)}, bf16[272,256]{1,0:T(8,128)(2,1)S(1)}, u32[]{:S(2)}, u32[]{:S(2)}) %collective-permute-start.6) | collective-permute-done | bytes 139296 | tf_op jit(solution)/shard_map/ppermute | solution.py:215
  41.7 3.6 %collective-permute-done.11.refs_7_ = bf16[272,256]{1,0:T(8,128)(2,1)S(1)} collective-permute-done((bf16[272,256]{1,0:T(8,128)(2,1)S(1)}, bf16[272,256]{1,0:T(8,128)(2,1)S(1)}, u32[]{:S(2)}, u32[]{:S(2)}) %collective-permute-start.11) | collective-permute-done | bytes 139296 | tf_op jit(solution)/shard_map/ppermute | solution.py:215
  45.3 1.9 %shard_map.53 = f32[3,65,1024]{2,1,0:T(8,128)} custom-call(s32[3]{0:T(128)S(1)} %copy-done.2, f32[272,256]{1,0:T(8,128)S(1)} %get-tuple-element.17.refs_0_, bf16[272,256]{1,0:T(8,128)(2,1)S(1)} %collective-permute-done.4.refs_1_, f32[272,256]{1,0:T(8,128)S(1)} %get-tuple-element.19.refs_2_, bf16[544,256]{1,0:T(8,128)(2,1)S(1)} %collective-permute-done.5.refs_3_, ...), custom_call_target="tpu_custom_call" | custom-call | flops 2000000000 | bytes 6000000 | tf_op jit(solution)/shard_map/pallas_call | solution.py:357
  (8 shorter events, 0.1 us)
Async XLA Ops:
  0.0 7.1 %copy-start.2 = (s32[3]{0:T(128)S(1)}, s32[3]{0:T(128)}, u32[]{:S(2)}) copy-start(s32[3]{0:T(128)} %masks_ref.5) | copy-start | bytes 40
  2.6 4.6 %collective-permute-start = (bf16[1024,128]{1,0:T(8,128)(2,1)}, bf16[1024,128]{1,0:T(8,128)(2,1)S(1)}, u32[]{:S(2)}, u32[]{:S(2)}) collective-permute-start(bf16[1024,128]{1,0:T(8,128)(2,1)} %shard_map.46.white_ref), channel_id=1, source_target_pairs={{0,4},{4,0},{8,12},{12,8},{16,20},{20,16},{24,28},{28,24},{1,5},{5... | collective-permute-start | bytes 786440 | tf_op jit(solution)/shard_map/ppermute | solution.py:215
  2.6 9.3 %collective-permute-start.2 = (bf16[1024,128]{1,0:T(8,128)(2,1)}, bf16[1024,128]{1,0:T(8,128)(2,1)S(1)}, u32[]{:S(2)}, u32[]{:S(2)}) collective-permute-start(bf16[1024,128]{1,0:T(8,128)(2,1)} %shard_map.46.white_ref), channel_id=1, source_target_pairs={{0,28},{4,24},{8,20},{12,16},{16,12},{20,8},{24,4},{28,0},{1,29},{... | collective-permute-start | bytes 786440 | tf_op jit(solution)/shard_map/ppermute | solution.py:215
  4.2 10.7 %collective-permute-start.1 = (bf16[1024,128]{1,0:T(8,128)(2,1)}, bf16[1024,128]{1,0:T(8,128)(2,1)S(1)}, u32[]{:S(2)}, u32[]{:S(2)}) collective-permute-start(bf16[1024,128]{1,0:T(8,128)(2,1)} %shard_map.46.white_ref), channel_id=1, source_target_pairs={{0,1},{1,0},{2,3},{3,2},{4,5},{5,4},{6,7},{7,6},{8,9},{9,8},{10,11... | collective-permute-start | bytes 786440 | tf_op jit(solution)/shard_map/ppermute | solution.py:215
  4.7 1.0 %copy-start = (bf16[1024,128]{1,0:T(8,128)(2,1)S(1)}, bf16[1024,128]{1,0:T(8,128)(2,1)}, u32[]{:S(2)}) copy-start(bf16[1024,128]{1,0:T(8,128)(2,1)} %shard_map.46.white_ref) | copy-start | bytes 786436
  5.7 1.5 %copy-start.1 = (bf16[1024,128]{1,0:T(8,128)(2,1)S(1)}, bf16[1024,128]{1,0:T(8,128)(2,1)}, u32[]{:S(2)}) copy-start(bf16[1024,128]{1,0:T(8,128)(2,1)} %shard_map.46.white_ref) | copy-start | bytes 786436
  7.7 10.4 %collective-permute-start.7 = (bf16[1024,128]{1,0:T(8,128)(2,1)S(1)}, bf16[1024,128]{1,0:T(8,128)(2,1)S(1)}, u32[]{:S(2)}, u32[]{:S(2)}) collective-permute-start(bf16[1024,128]{1,0:T(8,128)(2,1)S(1)} %shard_map.51), channel_id=1, source_target_pairs={{0,8},{4,12},{8,0},{12,4},{16,24},{20,28},{24,16},{28,20},{1,9},{5... | collective-permute-start | bytes 786440 | tf_op jit(solution)/shard_map/ppermute | solution.py:215
  9.3 8.8 %collective-permute-start.8 = (bf16[1024,128]{1,0:T(8,128)(2,1)S(1)}, bf16[1024,128]{1,0:T(8,128)(2,1)S(1)}, u32[]{:S(2)}, u32[]{:S(2)}) collective-permute-start(bf16[1024,128]{1,0:T(8,128)(2,1)S(1)} %shard_map.51), channel_id=1, source_target_pairs={{0,16},{4,20},{8,24},{12,28},{16,0},{20,4},{24,8},{28,12},{1,17},{... | collective-permute-start | bytes 786440 | tf_op jit(solution)/shard_map/ppermute | solution.py:215
  11.9 6.2 %collective-permute-start.9 = (bf16[1024,128]{1,0:T(8,128)(2,1)S(1)}, bf16[1024,128]{1,0:T(8,128)(2,1)S(1)}, u32[]{:S(2)}, u32[]{:S(2)}) collective-permute-start(bf16[1024,128]{1,0:T(8,128)(2,1)S(1)} %collective-permute-done.2.theirs_ref), channel_id=1, source_target_pairs={{0,4},{4,0},{8,12},{12,8},{16,20},{20,16},{24,28},{28,24},{1,5},{5... | collective-permute-start | bytes 786440 | tf_op jit(solution)/shard_map/ppermute | solution.py:215
  14.4 9.1 %collective-permute-start.5 = (bf16[544,256]{1,0:T(8,128)(2,1)S(1)}, bf16[544,256]{1,0:T(8,128)(2,1)S(1)}, u32[]{:S(2)}, u32[]{:S(2)}) collective-permute-start(bf16[544,256]{1,0:T(8,128)(2,1)S(1)} %get-tuple-element.15), channel_id=1, source_target_pairs={{0,1},{1,0},{2,3},{3,2},{4,5},{5,4},{6,7},{7,6},{8,9},{9,8},{10,11... | collective-permute-start | bytes 835592 | tf_op jit(solution)/shard_map/ppermute | solution.py:215
  14.9 6.1 %collective-permute-start.3 = (bf16[1024,128]{1,0:T(8,128)(2,1)S(1)}, bf16[1024,128]{1,0:T(8,128)(2,1)S(1)}, u32[]{:S(2)}, u32[]{:S(2)}) collective-permute-start(bf16[1024,128]{1,0:T(8,128)(2,1)S(1)} %collective-permute-done.1.white_ref), channel_id=1, source_target_pairs={{0,4},{4,0},{8,12},{12,8},{16,20},{20,16},{24,28},{28,24},{1,5},{5... | collective-permute-start | bytes 786440 | tf_op jit(solution)/shard_map/ppermute | solution.py:215
  20.2 19.0 %collective-permute-start.10 = (bf16[544,256]{1,0:T(8,128)(2,1)S(1)}, bf16[544,256]{1,0:T(8,128)(2,1)S(1)}, u32[]{:S(2)}, u32[]{:S(2)}) collective-permute-start(bf16[544,256]{1,0:T(8,128)(2,1)S(1)} %get-tuple-element.22), channel_id=1, source_target_pairs={{0,1},{1,0},{2,3},{3,2},{4,5},{5,4},{6,7},{7,6},{8,9},{9,8},{10,11... | collective-permute-start | bytes 835592 | tf_op jit(solution)/shard_map/ppermute | solution.py:215
  22.7 16.5 %collective-permute-start.4 = (bf16[272,256]{1,0:T(8,128)(2,1)S(1)}, bf16[272,256]{1,0:T(8,128)(2,1)S(1)}, u32[]{:S(2)}, u32[]{:S(2)}) collective-permute-start(bf16[272,256]{1,0:T(8,128)(2,1)S(1)} %get-tuple-element.18), channel_id=1, source_target_pairs={{0,2},{1,3},{2,0},{3,1},{4,6},{5,7},{6,4},{7,5},{8,10},{9,11},{10,... | collective-permute-start | bytes 417800 | tf_op jit(solution)/shard_map/ppermute | solution.py:215
  23.5 18.2 %collective-permute-start.6 = (bf16[272,256]{1,0:T(8,128)(2,1)S(1)}, bf16[272,256]{1,0:T(8,128)(2,1)S(1)}, u32[]{:S(2)}, u32[]{:S(2)}) collective-permute-start(bf16[272,256]{1,0:T(8,128)(2,1)S(1)} %add_convert_fusion.1), channel_id=1, source_target_pairs={{0,2},{1,3},{2,0},{3,1},{4,6},{5,7},{6,4},{7,5},{8,10},{9,11},{10,... | collective-permute-start | bytes 417800 | tf_op jit(solution)/shard_map/ppermute | solution.py:215
  39.3 6.0 %collective-permute-start.11 = (bf16[272,256]{1,0:T(8,128)(2,1)S(1)}, bf16[272,256]{1,0:T(8,128)(2,1)S(1)}, u32[]{:S(2)}, u32[]{:S(2)}) collective-permute-start(bf16[272,256]{1,0:T(8,128)(2,1)S(1)} %add_convert_fusion), channel_id=1, source_target_pairs={{0,2},{1,3},{2,0},{3,1},{4,6},{5,7},{6,4},{7,5},{8,10},{9,11},{10,... | collective-permute-start | bytes 417800 | tf_op jit(solution)/shard_map/ppermute | solution.py:215

commit v2 on v1

--- a/solution.py
+++ b/solution.py
@@ -20,6 +20,8 @@
 FAR_AFTER = False
 LAST_AFTER = 1
 LATE_Z = False
+FAR_FIRST = True
+EARLY = False
 NEAR_FIRST = False
 FAR, FREE = "low", "low"
 NT = (((1,), (1,)), ((), ()))
@@ -74,14 +76,12 @@
     for w in range(2):
         wide_ref[w, w * chans : (w + 1) * chans, :] = rec_ref[0, :, pl.ds(bases[w], CUT)]
     parts = []
-    for c in range(L // 256):
-        part = lax.dot_general(
-            bands[0], wide_ref[0, :, c * 256 : c * 256 + 512], NT, preferred_element_type=jnp.float32
-        )
-        part += lax.dot_general(
-            bands[1], wide_ref[1, :, c * 256 : c * 256 + 512], NT, preferred_element_type=jnp.float32
-        )
-        parts.append(part)
+    for c in range(0, L, 512):
+        pair = 0.0
+        for w in range(2):
+            both = jnp.concatenate([wide_ref[w, :, c : c + 512], wide_ref[w, :, c + 256 : c + 768]], axis=0)
+            pair += lax.dot_general(bands[w], both, NT, preferred_element_type=jnp.float32)
+        parts += [pair[:, 0:128], pair[:, 128:256]]
     power = sum(jnp.sum(part * part, axis=0, keepdims=True) for part in parts) * (1.0 / L)
     scale = lax.rsqrt(power + 1e-06)
     for c, part in enumerate(parts):
@@ -177,38 +177,44 @@
 
 
 def chosen_kernel(places, last, masks_ref, x_ref, y_ref, corner_ref, lhs_ref, *refs):
-    outs, w_ref, theirs_ref = refs[:-2], refs[-2], refs[-1]
-    chip = third_mask(masks_ref, last) >> 1
-    for k, ref in enumerate((x_ref, y_ref, corner_ref)):
-
-        @pl.when(chip == k + 1)
-        def _(ref=ref):
-            theirs_ref[...] = ref[...]
-
-    correlate(places, theirs_ref[...], lhs_ref, outs, w_ref)
-
-
-def finish_kernel(share, norm, last, counts, masks_ref, *refs):
-    ins, out_ref, s_ref = list(refs[:-2]), refs[-2], refs[-1]
+    outs, w_ref = refs[:-1], refs[-1]
+    masks = masks_ref[...]
+    chip = (masks[:, 0:1] ^ masks[:, 1:2] ^ masks[:, 2:3] ^ 1 ^ last) >> 1
+    x, y, corner = (ref[...].astype(jnp.float32) for ref in (x_ref, y_ref, corner_ref))
+    theirs = jnp.where(chip == 1, x, jnp.where(chip == 2, y, corner))
+    correlate(places, theirs, lhs_ref, outs, w_ref)
+
+
+def finish_kernel(share, norm, last, names, counts, masks_hbm, *refs):
+    ins, out_ref, s_ref, plane_ref, masks_ref, sems = list(refs[: sum(counts)]), *refs[-5:]
+    fetch = pltpu.make_async_copy(masks_hbm, masks_ref, sems.at[len(names)])
+    fetch.start()
     low = lax.broadcasted_iota(jnp.int32, (1, 128), 1) < 64
-    third = third_mask(masks_ref, last)
     rows = PLANES * share
-    for k, mask in enumerate((1, last, third)):
+    copies = []
+    for k, name in enumerate(names):
         total = sum(ins.pop(0)[0:rows, :].astype(jnp.float32) for _ in range(counts[k])) * norm
         s_ref[0] = total[:, 0:128]
         s_ref[1] = total[:, 128:256]
-        r = jnp.where(masks_ref[0] == mask, 0, jnp.where(masks_ref[1] == mask, 1, 2))
         for pair in range(share // 2):
             to = slice(pair * 128, pair * 128 + 128)
             for tile in range(COARSE // 2):
                 one = s_ref[tile, pl.ds(2 * pair, FINE, stride=share), :]
                 two = s_ref[tile, pl.ds(2 * pair + 1, FINE, stride=share), :]
                 q = 2 * tile * FINE
-                out_ref[r, q : q + FINE, to] = jnp.where(low, one, pltpu.roll(two, 64, 1))
-                out_ref[r, q + FINE : q + 2 * FINE, to] = jnp.where(low, pltpu.roll(one, 64, 1), two)
+                plane_ref[k, q : q + FINE, to] = jnp.where(low, one, pltpu.roll(two, 64, 1))
+                plane_ref[k, q + FINE : q + 2 * FINE, to] = jnp.where(low, pltpu.roll(one, 64, 1), two)
             one = s_ref[1, FINE * share + 2 * pair : FINE * share + 2 * pair + 1, :]
             two = s_ref[1, FINE * share + 2 * pair + 1 : FINE * share + 2 * pair + 2, :]
-            out_ref[r, LAGS - 1 : LAGS, to] = jnp.where(low, pltpu.roll(one, 64, 1), two)
+            plane_ref[k, LAGS - 1 : LAGS, to] = jnp.where(low, pltpu.roll(one, 64, 1), two)
+        if k == 0:
+            fetch.wait()
+        mask = {"near": 1, "far": last, "third": third_mask(masks_ref, last)}[name]
+        r = jnp.where(masks_ref[0] == mask, 0, jnp.where(masks_ref[1] == mask, 1, 2))
+        copies.append(pltpu.make_async_copy(plane_ref.at[k], out_ref.at[r], sems.at[k]))
+        copies[-1].start()
+    for copy in copies:
+        copy.wait()
 
 
 def apart(value, axis, mask):
@@ -251,7 +257,7 @@
             micros=1.5,
         )(block)
 
-    lhs = prepare(white, days)
+    lhs = prepare(lax.optimization_barrier((white, near))[0] if EARLY else white, days)
 
     slot_rows = PLANES * share
     weights = pltpu.VMEM((2 * PAD, 256), bf16)
@@ -307,10 +313,10 @@
             parts = call(
                 functools.partial(chosen_kernel, places, last),
                 shapes,
-                [SMEM] + [VMEM] * (len(theirs) + 1),
-                [weights, pltpu.VMEM((L, 2 * chans), bf16)],
+                [VMEM] * (len(theirs) + 2),
+                [weights],
                 micros=2.0,
-            )(pick, *theirs, lhs)
+            )(pick.reshape(1, -1), *theirs, lhs)
         return parts[-1], started(mode, steps, outs, parts)
 
     if blocks == 8:
@@ -324,7 +330,8 @@
         along_y = apart(passed, "chan", 4)
     far_done, far_sum = day_sum(FAR, far)
     if days == 4:
-        white2, _ = lax.optimization_barrier((white2, far_done))
+        if FAR_FIRST:
+            white2, _ = lax.optimization_barrier((white2, far_done))
         near2 = apart(white2, "chan", 1)
         near_kept, near_done = call(
             paired_kernel,
@@ -353,14 +360,27 @@
 
     day_total = records.shape[0] * days
     norm = float((day_total * window_offsets.shape[1] * L) ** -0.5)
-    flat = [part for group in sums for part in group]
-    return call(
-        functools.partial(finish_kernel, share, norm, last, [len(group) for group in sums]),
-        jax.ShapeDtypeStruct((3, LAGS, share * chans), f32),
-        [SMEM] + [VMEM] * len(flat),
-        [pltpu.VMEM((2, slot_rows, 128), f32)],
-        micros=2.0,
-    )(pair_masks, *flat)
+
+    def finish(names, groups, before=None):
+        flat = [part for group in groups for part in group]
+        extra = [] if before is None else [before]
+        return pl.pallas_call(
+            functools.partial(finish_kernel, share, norm, last, names, [len(group) for group in groups]),
+            out_shape=jax.ShapeDtypeStruct((3, LAGS, share * chans), f32),
+            in_specs=[HBM] + [VMEM] * len(flat) + [HBM] * len(extra),
+            out_specs=HBM,
+            scratch_shapes=[
+                pltpu.VMEM((2, slot_rows, 128), f32),
+                pltpu.VMEM((len(names), LAGS, share * chans), f32),
+                pltpu.SMEM(pair_masks.shape, jnp.int32),
+                pltpu.SemaphoreType.DMA((len(names) + 1,)),
+            ],
+            input_output_aliases={1 + len(flat): 0} if extra else {},
+            compiler_params=pltpu.CompilerParams(vmem_limit_bytes=24 * 1024 * 1024),
+            cost_estimate=pl.CostEstimate(flops=int(1e9), bytes_accessed=int(3e6), transcendentals=0),
+        )(pair_masks, *flat, *extra)
+
+    return finish(["third"], sums[2:], finish(["near", "far"], sums[:2]))
 
 
 def solution(mesh):

time: 47.4 us -> 46.9 us (0.989)
  the two profiles are of different devices: /device:TPU:26 before, /device:TPU:0 now
where the time goes in v2:
time: 46.9 us; the launch traced here: 46.8 us
  waiting for transfers between devices  16.9 us (36%)
  starting transfers between devices  15.7 us (33%)
  Pallas kernels  13 us (28%)
  local copies, waits for them, and re-layouts  0.99 us (2%)
    ppermute x12, waiting for transfers between devices, apart(): lax.ppermute(value, axis, [(s, s ^ mask) for s in range(lax.axis_size(axi...  16.9 us
    ppermute x12, starting transfers between devices, apart(): lax.ppermute(value, axis, [(s, s ^ mask) for s in range(lax.axis_size(axi...  15.7 us
    pallas_call x2, Pallas kernels, finish(): pl.pallas_call(functools.partial(finish_kernel, share, norm, last, names,...  2.89 us
    pallas_call x1, Pallas kernels, local(): call(whiten_kernel, jax.ShapeDtypeStruct((L, 2 * chans), bf16), [HBM] * 3...  2.31 us
    pallas_call x2, Pallas kernels, prepare(): call(functools.partial(prepare_kernel, days, count), jax.ShapeDtypeStruct...  2.24 us
    pallas_call x1, Pallas kernels, day_sum(): call(functools.partial(chosen_kernel, places, last), shapes, [VMEM] * (le...  1.75 us
    pallas_call x1, Pallas kernels, local(): call(paired_kernel, [jax.ShapeDtypeStruct((slot_rows, 256), f32), jax.Sha...  1.69 us
    pallas_call x1, Pallas kernels, day_sum(): call(functools.partial(known_kernel, places), shapes, [VMEM] * 2, [weight...  1.58 us
  transfers between devices with their start and end apart: 12, of which 6 were waited for; matrix products, arithmetic and copies ran while one was open for 0% of the time, Pallas kernels for 20%

profile of v2, /device:TPU:0, one launch (start us, length us, event | category | flops | bytes accessed | tf_op | source)
XLA Modules:
  0.0 46.8 jit_solution(15247349077427447187)
XLA Ops:
  0.0 2.3 %shard_map.46.white_ref = bf16[1024,128]{1,0:T(8,128)(2,1)} custom-call(s32[1,2]{1,0:T(1,128)} %off_hbm.1, bf16[1,64]{1,0:T(2,128)(2,1)} %bitcast.3, bf16[1,64,4096]{2,1,0:T(8,128)(2,1)} %rec_hbm.1), custom_call_target="tpu_custom_call" | custom-call | flops 2000000000 | bytes 6000000 | tf_op jit(solution)/shard_map/pallas_call | solution.py:232
  2.3 0.5 %collective-permute-start = (bf16[1024,128]{1,0:T(8,128)(2,1)}, bf16[1024,128]{1,0:T(8,128)(2,1)S(1)}, u32[]{:S(2)}, u32[]{:S(2)}) collective-permute-start(bf16[1024,128]{1,0:T(8,128)(2,1)} %shard_map.46.white_ref), channel_id=1, source_target_pairs={{0,4},{4,0},{8,12},{12,8},{16,20},{20,16},{24,28},{28,24},{1,5},{5... | collective-permute-start | bytes 786440 | tf_op jit(solution)/shard_map/ppermute | solution.py:221
  2.8 3.6 %collective-permute-start.3 = (bf16[1024,128]{1,0:T(8,128)(2,1)}, bf16[1024,128]{1,0:T(8,128)(2,1)S(1)}, u32[]{:S(2)}, u32[]{:S(2)}) collective-permute-start(bf16[1024,128]{1,0:T(8,128)(2,1)} %shard_map.46.white_ref), channel_id=1, source_target_pairs={{0,28},{4,24},{8,20},{12,16},{16,12},{20,8},{24,4},{28,0},{1,29},{... | collective-permute-start | bytes 786440 | tf_op jit(solution)/shard_map/ppermute | solution.py:221
  6.4 1.6 %collective-permute-start.6 = (bf16[1024,128]{1,0:T(8,128)(2,1)}, bf16[1024,128]{1,0:T(8,128)(2,1)S(1)}, u32[]{:S(2)}, u32[]{:S(2)}) collective-permute-start(bf16[1024,128]{1,0:T(8,128)(2,1)} %shard_map.46.white_ref), channel_id=1, source_target_pairs={{0,1},{1,0},{2,3},{3,2},{4,5},{5,4},{6,7},{7,6},{8,9},{9,8},{10,11... | collective-permute-start | bytes 786440 | tf_op jit(solution)/shard_map/ppermute | solution.py:221
  8.0 1.0 %copy-done = bf16[1024,128]{1,0:T(8,128)(2,1)S(1)} copy-done((bf16[1024,128]{1,0:T(8,128)(2,1)S(1)}, bf16[1024,128]{1,0:T(8,128)(2,1)}, u32[]{:S(2)}) %copy-start) | copy-done | bytes 262168
  9.0 1.4 %shard_map.48.lhs_ref = bf16[1088,2304]{1,0:T(8,128)(2,1)S(1)} custom-call(bf16[1024,128]{1,0:T(8,128)(2,1)S(1)} %copy-done), custom_call_target="tpu_custom_call" | custom-call | flops 1500000000 | bytes 4500000 | tf_op jit(solution)/shard_map/pallas_call | solution.py:253
  10.4 0.0 collective-permute-done.near_ref.theirs_ref
  10.4 0.6 %shard_map.47 = bf16[1024,128]{1,0:T(8,128)(2,1)S(1)} custom-call(s32[3]{0:T(128)S(1)} %copy-done.2, bf16[1024,128]{1,0:T(8,128)(2,1)S(1)} %copy-done.1, bf16[1024,128]{1,0:T(8,128)(2,1)S(1)} %collective-permute-done.near_ref.theirs_ref), custom_call_target="tpu_custom_call" | custom-call | flops 500000000 | bytes 1500000 | tf_op jit(solution)/shard_map/pallas_call | solution.py:323
  11.0 0.6 %collective-permute-start.1 = (bf16[1024,128]{1,0:T(8,128)(2,1)S(1)}, bf16[1024,128]{1,0:T(8,128)(2,1)S(1)}, u32[]{:S(2)}, u32[]{:S(2)}) collective-permute-start(bf16[1024,128]{1,0:T(8,128)(2,1)S(1)} %shard_map.47), channel_id=1, source_target_pairs={{0,8},{4,12},{8,0},{12,4},{16,24},{20,28},{24,16},{28,20},{1,9},{5... | collective-permute-start | bytes 786440 | tf_op jit(solution)/shard_map/ppermute | solution.py:221
  11.6 0.5 %collective-permute-start.2 = (bf16[1024,128]{1,0:T(8,128)(2,1)S(1)}, bf16[1024,128]{1,0:T(8,128)(2,1)S(1)}, u32[]{:S(2)}, u32[]{:S(2)}) collective-permute-start(bf16[1024,128]{1,0:T(8,128)(2,1)S(1)} %shard_map.47), channel_id=1, source_target_pairs={{0,16},{4,20},{8,24},{12,28},{16,0},{20,4},{24,8},{28,12},{1,17},{... | collective-permute-start | bytes 786440 | tf_op jit(solution)/shard_map/ppermute | solution.py:221
  12.1 1.3 %collective-permute-done.3.theirs_ref = bf16[1024,128]{1,0:T(8,128)(2,1)S(1)} collective-permute-done((bf16[1024,128]{1,0:T(8,128)(2,1)}, bf16[1024,128]{1,0:T(8,128)(2,1)S(1)}, u32[]{:S(2)}, u32[]{:S(2)}) %collective-permute-start.3) | collective-permute-done | bytes 262176 | tf_op jit(solution)/shard_map/ppermute | solution.py:221
  13.4 0.0 collective-permute-start.4
  13.4 1.6 %shard_map.50 = (f32[272,256]{1,0:T(8,128)S(1)}, f32[272,256]{1,0:T(8,128)S(1)}, bf16[544,256]{1,0:T(8,128)(2,1)S(1)}) custom-call(bf16[1024,128]{1,0:T(8,128)(2,1)S(1)} %collective-permute-done.3.theirs_ref, bf16[1088,2304]{1,0:T(8,128)(2,1)S(1)} %shard_map.48.lhs_ref), custom_call_target="tpu_custom_call" | custom-call | flops 2000000000 | bytes 6000000 | tf_op jit(solution)/shard_map/pallas_call | solution.py:311
  15.0 2.3 %collective-permute-start.10 = (bf16[544,256]{1,0:T(8,128)(2,1)S(1)}, bf16[544,256]{1,0:T(8,128)(2,1)S(1)}, u32[]{:S(2)}, u32[]{:S(2)}) collective-permute-start(bf16[544,256]{1,0:T(8,128)(2,1)S(1)} %get-tuple-element.17), channel_id=1, source_target_pairs={{0,1},{1,0},{2,3},{3,2},{4,5},{5,4},{6,7},{7,6},{8,9},{9,8},{10,11... | collective-permute-start | bytes 835592 | tf_op jit(solution)/shard_map/ppermute | solution.py:221
  17.2 0.0 collective-permute-done.6.white_ref
  17.3 0.0 collective-permute-start.7
  17.3 0.8 %shard_map.51.lhs2_ref = bf16[544,2304]{1,0:T(8,128)(2,1)S(1)} custom-call(bf16[1024,128]{1,0:T(8,128)(2,1)S(1)} %collective-permute-done.6.white_ref), custom_call_target="tpu_custom_call" | custom-call | flops 1500000000 | bytes 4500000 | tf_op jit(solution)/shard_map/pallas_call | solution.py:253
  18.1 1.2 %collective-permute-done.1.x_ref = bf16[1024,128]{1,0:T(8,128)(2,1)S(1)} collective-permute-done((bf16[1024,128]{1,0:T(8,128)(2,1)S(1)}, bf16[1024,128]{1,0:T(8,128)(2,1)S(1)}, u32[]{:S(2)}, u32[]{:S(2)}) %collective-permute-start.1) | collective-permute-done | bytes 262176 | tf_op jit(solution)/shard_map/ppermute | solution.py:221
  19.3 0.0 collective-permute-done.2.y_ref
  19.3 0.0 collective-permute-done.4.corner_ref
  19.3 1.8 %shard_map.49 = (f32[272,256]{1,0:T(8,128)S(1)}, f32[272,256]{1,0:T(8,128)S(1)}, bf16[544,256]{1,0:T(8,128)(2,1)S(1)}) custom-call(s32[1,3]{1,0:T(1,128)S(1)} %bitcast.2, bf16[1024,128]{1,0:T(8,128)(2,1)S(1)} %collective-permute-done.1.x_ref, bf16[1024,128]{1,0:T(8,128)(2,1)S(1)} %collective-permute-done.2.y_ref, ...), custom_call_target="tpu_custom_call" | custom-call | flops 2000000000 | bytes 6000000 | tf_op jit(solution)/shard_map/pallas_call | solution.py:313
  21.1 1.6 %collective-permute-start.5 = (bf16[544,256]{1,0:T(8,128)(2,1)S(1)}, bf16[544,256]{1,0:T(8,128)(2,1)S(1)}, u32[]{:S(2)}, u32[]{:S(2)}) collective-permute-start(bf16[544,256]{1,0:T(8,128)(2,1)S(1)} %get-tuple-element.16), channel_id=1, source_target_pairs={{0,1},{1,0},{2,3},{3,2},{4,5},{5,4},{6,7},{7,6},{8,9},{9,8},{10,11... | collective-permute-start | bytes 835592 | tf_op jit(solution)/shard_map/ppermute | solution.py:221
  22.7 1.7 %shard_map.52 = (f32[272,256]{1,0:T(8,128)S(1)}, bf16[272,256]{1,0:T(8,128)(2,1)S(1)}) custom-call(bf16[1024,128]{1,0:T(8,128)(2,1)S(1)} %collective-permute-done.near_ref.theirs_ref, bf16[1088,2304]{1,0:T(8,128)(2,1)S(1)} %shard_map.48.lhs_ref, bf16[1024,128]{1,0:T(8,128)(2,1)S(1)} %collective-permute-done.7.theirs2_ref, ...), custom_call_target="tpu_custom_call" | custom-call | flops 2000000000 | bytes 6000000 | tf_op jit(solution)/shard_map/pallas_call | solution.py:336
  24.4 2.6 %collective-permute-start.8 = (bf16[272,256]{1,0:T(8,128)(2,1)S(1)}, bf16[272,256]{1,0:T(8,128)(2,1)S(1)}, u32[]{:S(2)}, u32[]{:S(2)}) collective-permute-start(bf16[272,256]{1,0:T(8,128)(2,1)S(1)} %get-tuple-element.19), channel_id=1, source_target_pairs={{0,2},{1,3},{2,0},{3,1},{4,6},{5,7},{6,4},{7,5},{8,10},{9,11},{10,... | collective-permute-start | bytes 417800 | tf_op jit(solution)/shard_map/ppermute | solution.py:221
  27.1 0.4 collective-permute-start.11
  27.5 5.7 %collective-permute-done.8.refs_1_ = bf16[272,256]{1,0:T(8,128)(2,1)S(1)} collective-permute-done((bf16[272,256]{1,0:T(8,128)(2,1)S(1)}, bf16[272,256]{1,0:T(8,128)(2,1)S(1)}, u32[]{:S(2)}, u32[]{:S(2)}) %collective-permute-start.8) | collective-permute-done | bytes 139296 | tf_op jit(solution)/shard_map/ppermute | solution.py:221
  33.2 1.6 %collective-permute-done.5.refs_1_ = bf16[544,256]{1,0:T(8,128)(2,1)S(1)} collective-permute-done((bf16[544,256]{1,0:T(8,128)(2,1)S(1)}, bf16[544,256]{1,0:T(8,128)(2,1)S(1)}, u32[]{:S(2)}, u32[]{:S(2)}) %collective-permute-start.5) | collective-permute-done | bytes 278560 | tf_op jit(solution)/shard_map/ppermute | solution.py:221
  34.8 1.9 %collective-permute-start.9 = (bf16[272,256]{1,0:T(8,128)(2,1)S(1)}, bf16[272,256]{1,0:T(8,128)(2,1)S(1)}, u32[]{:S(2)}, u32[]{:S(2)}) collective-permute-start(bf16[272,256]{1,0:T(8,128)(2,1)S(1)} %add_convert_fusion.1), channel_id=1, source_target_pairs={{0,2},{1,3},{2,0},{3,1},{4,6},{5,7},{6,4},{7,5},{8,10},{9,11},{10,... | collective-permute-start | bytes 417800 | tf_op jit(solution)/shard_map/ppermute | solution.py:221
  36.7 5.3 %collective-permute-done.11.refs_4_ = bf16[272,256]{1,0:T(8,128)(2,1)S(1)} collective-permute-done((bf16[272,256]{1,0:T(8,128)(2,1)S(1)}, bf16[272,256]{1,0:T(8,128)(2,1)S(1)}, u32[]{:S(2)}, u32[]{:S(2)}) %collective-permute-start.11) | collective-permute-done | bytes 139296 | tf_op jit(solution)/shard_map/ppermute | solution.py:221
  42.0 1.5 %shard_map.53.refs_3_ = f32[3,65,1024]{2,1,0:T(8,128)} custom-call(s32[3]{0:T(128)S(1)} %copy-done.2, f32[272,256]{1,0:T(8,128)S(1)} %get-tuple-element.22.refs_0_, bf16[272,256]{1,0:T(8,128)(2,1)S(1)} %collective-permute-done.8.refs_1_, f32[272,256]{1,0:T(8,128)S(1)} %get-tuple-element.23.refs_2_, bf16[544,256]{1,0:T(8,128)(2,1)S(1)} %collective-permute-done.10.refs_3_, ...), custom_call_target="tpu_custom_call" | custom-call | flops 1000000000 | bytes 3000000 | tf_op jit(solution)/shard_map/pallas_call | solution.py:367
  43.5 1.9 %collective-permute-done.9.refs_2_ = bf16[272,256]{1,0:T(8,128)(2,1)S(1)} collective-permute-done((bf16[272,256]{1,0:T(8,128)(2,1)S(1)}, bf16[272,256]{1,0:T(8,128)(2,1)S(1)}, u32[]{:S(2)}, u32[]{:S(2)}) %collective-permute-start.9) | collective-permute-done | bytes 139296 | tf_op jit(solution)/shard_map/ppermute | solution.py:221
  45.4 1.4 %shard_map.54 = f32[3,65,1024]{2,1,0:T(8,128)} custom-call(s32[3]{0:T(128)S(1)} %copy-done.2, f32[272,256]{1,0:T(8,128)S(1)} %get-tuple-element.15.refs_0_, bf16[544,256]{1,0:T(8,128)(2,1)S(1)} %collective-permute-done.5.refs_1_, bf16[272,256]{1,0:T(8,128)(2,1)S(1)} %collective-permute-done.9.refs_2_, ...), custom_call_target="tpu_custom_call", output_to_operand_aliasing={{}: (4, {})} | custom-call | flops 1000000000 | bytes 3000000 | tf_op jit(solution)/shard_map/pallas_call | solution.py:367
  (9 shorter events, 0.1 us)
Async XLA Ops:
  0.0 10.4 %copy-start.2 = (s32[3]{0:T(128)S(1)}, s32[3]{0:T(128)}, u32[]{:S(2)}) copy-start(s32[3]{0:T(128)} %masks_hbm.3) | copy-start | bytes 40
  2.3 8.1 %collective-permute-start = (bf16[1024,128]{1,0:T(8,128)(2,1)}, bf16[1024,128]{1,0:T(8,128)(2,1)S(1)}, u32[]{:S(2)}, u32[]{:S(2)}) collective-permute-start(bf16[1024,128]{1,0:T(8,128)(2,1)} %shard_map.46.white_ref), channel_id=1, source_target_pairs={{0,4},{4,0},{8,12},{12,8},{16,20},{20,16},{24,28},{28,24},{1,5},{5... | collective-permute-start | bytes 786440 | tf_op jit(solution)/shard_map/ppermute | solution.py:221
  2.8 10.5 %collective-permute-start.3 = (bf16[1024,128]{1,0:T(8,128)(2,1)}, bf16[1024,128]{1,0:T(8,128)(2,1)S(1)}, u32[]{:S(2)}, u32[]{:S(2)}) collective-permute-start(bf16[1024,128]{1,0:T(8,128)(2,1)} %shard_map.46.white_ref), channel_id=1, source_target_pairs={{0,28},{4,24},{8,20},{12,16},{16,12},{20,8},{24,4},{28,0},{1,29},{... | collective-permute-start | bytes 786440 | tf_op jit(solution)/shard_map/ppermute | solution.py:221
  6.4 10.8 %collective-permute-start.6 = (bf16[1024,128]{1,0:T(8,128)(2,1)}, bf16[1024,128]{1,0:T(8,128)(2,1)S(1)}, u32[]{:S(2)}, u32[]{:S(2)}) collective-permute-start(bf16[1024,128]{1,0:T(8,128)(2,1)} %shard_map.46.white_ref), channel_id=1, source_target_pairs={{0,1},{1,0},{2,3},{3,2},{4,5},{5,4},{6,7},{7,6},{8,9},{9,8},{10,11... | collective-permute-start | bytes 786440 | tf_op jit(solution)/shard_map/ppermute | solution.py:221
  8.0 1.0 %copy-start = (bf16[1024,128]{1,0:T(8,128)(2,1)S(1)}, bf16[1024,128]{1,0:T(8,128)(2,1)}, u32[]{:S(2)}) copy-start(bf16[1024,128]{1,0:T(8,128)(2,1)} %shard_map.46.white_ref) | copy-start | bytes 786436
  9.0 1.5 %copy-start.1 = (bf16[1024,128]{1,0:T(8,128)(2,1)S(1)}, bf16[1024,128]{1,0:T(8,128)(2,1)}, u32[]{:S(2)}) copy-start(bf16[1024,128]{1,0:T(8,128)(2,1)} %shard_map.46.white_ref) | copy-start | bytes 786436
  11.0 8.3 %collective-permute-start.1 = (bf16[1024,128]{1,0:T(8,128)(2,1)S(1)}, bf16[1024,128]{1,0:T(8,128)(2,1)S(1)}, u32[]{:S(2)}, u32[]{:S(2)}) collective-permute-start(bf16[1024,128]{1,0:T(8,128)(2,1)S(1)} %shard_map.47), channel_id=1, source_target_pairs={{0,8},{4,12},{8,0},{12,4},{16,24},{20,28},{24,16},{28,20},{1,9},{5... | collective-permute-start | bytes 786440 | tf_op jit(solution)/shard_map/ppermute | solution.py:221
  11.6 7.7 %collective-permute-start.2 = (bf16[1024,128]{1,0:T(8,128)(2,1)S(1)}, bf16[1024,128]{1,0:T(8,128)(2,1)S(1)}, u32[]{:S(2)}, u32[]{:S(2)}) collective-permute-start(bf16[1024,128]{1,0:T(8,128)(2,1)S(1)} %shard_map.47), channel_id=1, source_target_pairs={{0,16},{4,20},{8,24},{12,28},{16,0},{20,4},{24,8},{28,12},{1,17},{... | collective-permute-start | bytes 786440 | tf_op jit(solution)/shard_map/ppermute | solution.py:221
  13.4 6.0 %collective-permute-start.4 = (bf16[1024,128]{1,0:T(8,128)(2,1)S(1)}, bf16[1024,128]{1,0:T(8,128)(2,1)S(1)}, u32[]{:S(2)}, u32[]{:S(2)}) collective-permute-start(bf16[1024,128]{1,0:T(8,128)(2,1)S(1)} %collective-permute-done.3.theirs_ref), channel_id=1, source_target_pairs={{0,4},{4,0},{8,12},{12,8},{16,20},{20,16},{24,28},{28,24},{1,5},{5... | collective-permute-start | bytes 786440 | tf_op jit(solution)/shard_map/ppermute | solution.py:221
  15.0 12.1 %collective-permute-start.10 = (bf16[544,256]{1,0:T(8,128)(2,1)S(1)}, bf16[544,256]{1,0:T(8,128)(2,1)S(1)}, u32[]{:S(2)}, u32[]{:S(2)}) collective-permute-start(bf16[544,256]{1,0:T(8,128)(2,1)S(1)} %get-tuple-element.17), channel_id=1, source_target_pairs={{0,1},{1,0},{2,3},{3,2},{4,5},{5,4},{6,7},{7,6},{8,9},{9,8},{10,11... | collective-permute-start | bytes 835592 | tf_op jit(solution)/shard_map/ppermute | solution.py:221
  17.3 5.5 %collective-permute-start.7 = (bf16[1024,128]{1,0:T(8,128)(2,1)S(1)}, bf16[1024,128]{1,0:T(8,128)(2,1)S(1)}, u32[]{:S(2)}, u32[]{:S(2)}) collective-permute-start(bf16[1024,128]{1,0:T(8,128)(2,1)S(1)} %collective-permute-done.6.white_ref), channel_id=1, source_target_pairs={{0,4},{4,0},{8,12},{12,8},{16,20},{20,16},{24,28},{28,24},{1,5},{5... | collective-permute-start | bytes 786440 | tf_op jit(solution)/shard_map/ppermute | solution.py:221
  21.1 13.7 %collective-permute-start.5 = (bf16[544,256]{1,0:T(8,128)(2,1)S(1)}, bf16[544,256]{1,0:T(8,128)(2,1)S(1)}, u32[]{:S(2)}, u32[]{:S(2)}) collective-permute-start(bf16[544,256]{1,0:T(8,128)(2,1)S(1)} %get-tuple-element.16), channel_id=1, source_target_pairs={{0,1},{1,0},{2,3},{3,2},{4,5},{5,4},{6,7},{7,6},{8,9},{9,8},{10,11... | collective-permute-start | bytes 835592 | tf_op jit(solution)/shard_map/ppermute | solution.py:221
  24.4 8.8 %collective-permute-start.8 = (bf16[272,256]{1,0:T(8,128)(2,1)S(1)}, bf16[272,256]{1,0:T(8,128)(2,1)S(1)}, u32[]{:S(2)}, u32[]{:S(2)}) collective-permute-start(bf16[272,256]{1,0:T(8,128)(2,1)S(1)} %get-tuple-element.19), channel_id=1, source_target_pairs={{0,2},{1,3},{2,0},{3,1},{4,6},{5,7},{6,4},{7,5},{8,10},{9,11},{10,... | collective-permute-start | bytes 417800 | tf_op jit(solution)/shard_map/ppermute | solution.py:221
  27.1 14.9 %collective-permute-start.11 = (bf16[272,256]{1,0:T(8,128)(2,1)S(1)}, bf16[272,256]{1,0:T(8,128)(2,1)S(1)}, u32[]{:S(2)}, u32[]{:S(2)}) collective-permute-start(bf16[272,256]{1,0:T(8,128)(2,1)S(1)} %add_convert_fusion), channel_id=1, source_target_pairs={{0,2},{1,3},{2,0},{3,1},{4,6},{5,7},{6,4},{7,5},{8,10},{9,11},{10,... | collective-permute-start | bytes 417800 | tf_op jit(solution)/shard_map/ppermute | solution.py:221
  34.8 10.5 %collective-permute-start.9 = (bf16[272,256]{1,0:T(8,128)(2,1)S(1)}, bf16[272,256]{1,0:T(8,128)(2,1)S(1)}, u32[]{:S(2)}, u32[]{:S(2)}) collective-permute-start(bf16[272,256]{1,0:T(8,128)(2,1)S(1)} %add_convert_fusion.1), channel_id=1, source_target_pairs={{0,2},{1,3},{2,0},{3,1},{4,6},{5,7},{6,4},{7,5},{8,10},{9,11},{10,... | collective-permute-start | bytes 417800 | tf_op jit(solution)/shard_map/ppermute | solution.py:221

commit v3 on v2

--- a/solution.py
+++ b/solution.py
@@ -15,7 +15,7 @@
 PLANES = FINE + 1
 PAD = 1152
 CUT = 1280
-COST = 1.0
+COST = 3.0
 DIRECT_ORDER = (2, 3, 1)
 FAR_AFTER = False
 LAST_AFTER = 1

time: 46.9 us -> 46 us (0.981)
  waiting for transfers between devices: 16.9 us -> 14.8 us
  starting transfers between devices: 15.7 us -> 16.6 us
    ppermute x12, waiting for transfers between devices: 16.9 us -> 14.8 us  [apart(): lax.ppermute(value, axis, [(s, s ^ mask) for s in range(lax.axis_size(axi...]
    ppermute x12, starting transfers between devices: 15.7 us -> 16.6 us  [apart(): lax.ppermute(value, axis, [(s, s ^ mask) for s in range(lax.axis_size(axi...]
  transfers between devices with their start and end apart: 12 -> 12, of which waited for: 6 -> 7; matrix products, arithmetic and copies ran while one was open for 0% -> 0% of each run, Pallas kernels for 20% -> 20%
where the time goes in v3:
time: 46 us; the launch traced here: 45.6 us
  starting transfers between devices  16.6 us (36%)
  waiting for transfers between devices  14.8 us (32%)
  Pallas kernels  13 us (28%)
  local copies, waits for them, and re-layouts  0.96 us (2%)
    ppermute x12, starting transfers between devices, apart(): lax.ppermute(value, axis, [(s, s ^ mask) for s in range(lax.axis_size(axi...  16.6 us
    ppermute x12, waiting for transfers between devices, apart(): lax.ppermute(value, axis, [(s, s ^ mask) for s in range(lax.axis_size(axi...  14.8 us
    pallas_call x2, Pallas kernels, finish(): pl.pallas_call(functools.partial(finish_kernel, share, norm, last, names,...  2.88 us
    pallas_call x1, Pallas kernels, local(): call(whiten_kernel, jax.ShapeDtypeStruct((L, 2 * chans), bf16), [HBM] * 3...  2.31 us
    pallas_call x2, Pallas kernels, prepare(): call(functools.partial(prepare_kernel, days, count), jax.ShapeDtypeStruct...  2.24 us
    pallas_call x1, Pallas kernels, day_sum(): call(functools.partial(chosen_kernel, places, last), shapes, [VMEM] * (le...  1.75 us
    pallas_call x1, Pallas kernels, local(): call(paired_kernel, [jax.ShapeDtypeStruct((slot_rows, 256), f32), jax.Sha...  1.69 us
    pallas_call x1, Pallas kernels, day_sum(): call(functools.partial(known_kernel, places), shapes, [VMEM] * 2, [weight...  1.57 us
  transfers between devices with their start and end apart: 12, of which 7 were waited for; matrix products, arithmetic and copies ran while one was open for 0% of the time, Pallas kernels for 20%

profile of v3, /device:TPU:0, one launch (start us, length us, event | category | flops | bytes accessed | tf_op | source)
XLA Modules:
  0.0 45.6 jit_solution(5631212814374047207)
XLA Ops:
  0.0 2.3 %shard_map.46.white_ref = bf16[1024,128]{1,0:T(8,128)(2,1)} custom-call(s32[1,2]{1,0:T(1,128)} %off_hbm.1, bf16[1,64]{1,0:T(2,128)(2,1)} %bitcast.3, bf16[1,64,4096]{2,1,0:T(8,128)(2,1)} %rec_hbm.1), custom_call_target="tpu_custom_call" | custom-call | flops 6000000000 | bytes 18000000 | tf_op jit(solution)/shard_map/pallas_call | solution.py:232
  2.3 3.4 %collective-permute-start.3 = (bf16[1024,128]{1,0:T(8,128)(2,1)}, bf16[1024,128]{1,0:T(8,128)(2,1)S(1)}, u32[]{:S(2)}, u32[]{:S(2)}) collective-permute-start(bf16[1024,128]{1,0:T(8,128)(2,1)} %shard_map.46.white_ref), channel_id=1, source_target_pairs={{0,28},{4,24},{8,20},{12,16},{16,12},{20,8},{24,4},{28,0},{1,29},{... | collective-permute-start | bytes 786440 | tf_op jit(solution)/shard_map/ppermute | solution.py:221
  5.7 1.6 %collective-permute-start.6 = (bf16[1024,128]{1,0:T(8,128)(2,1)}, bf16[1024,128]{1,0:T(8,128)(2,1)S(1)}, u32[]{:S(2)}, u32[]{:S(2)}) collective-permute-start(bf16[1024,128]{1,0:T(8,128)(2,1)} %shard_map.46.white_ref), channel_id=1, source_target_pairs={{0,1},{1,0},{2,3},{3,2},{4,5},{5,4},{6,7},{7,6},{8,9},{9,8},{10,11... | collective-permute-start | bytes 786440 | tf_op jit(solution)/shard_map/ppermute | solution.py:221
  7.3 0.4 collective-permute-start
  7.7 0.9 %copy-done = bf16[1024,128]{1,0:T(8,128)(2,1)S(1)} copy-done((bf16[1024,128]{1,0:T(8,128)(2,1)S(1)}, bf16[1024,128]{1,0:T(8,128)(2,1)}, u32[]{:S(2)}) %copy-start) | copy-done | bytes 262168
  8.7 1.4 %shard_map.48.lhs_ref = bf16[1088,2304]{1,0:T(8,128)(2,1)S(1)} custom-call(bf16[1024,128]{1,0:T(8,128)(2,1)S(1)} %copy-done), custom_call_target="tpu_custom_call" | custom-call | flops 4499999744 | bytes 13500000 | tf_op jit(solution)/shard_map/pallas_call | solution.py:253
  10.1 0.0 collective-permute-done.near_ref.theirs_ref
  10.1 0.6 %shard_map.47 = bf16[1024,128]{1,0:T(8,128)(2,1)S(1)} custom-call(s32[3]{0:T(128)S(1)} %copy-done.2, bf16[1024,128]{1,0:T(8,128)(2,1)S(1)} %copy-done.1, bf16[1024,128]{1,0:T(8,128)(2,1)S(1)} %collective-permute-done.near_ref.theirs_ref), custom_call_target="tpu_custom_call" | custom-call | flops 1500000000 | bytes 4500000 | tf_op jit(solution)/shard_map/pallas_call | solution.py:323
  10.7 0.6 %collective-permute-start.1 = (bf16[1024,128]{1,0:T(8,128)(2,1)S(1)}, bf16[1024,128]{1,0:T(8,128)(2,1)S(1)}, u32[]{:S(2)}, u32[]{:S(2)}) collective-permute-start(bf16[1024,128]{1,0:T(8,128)(2,1)S(1)} %shard_map.47), channel_id=1, source_target_pairs={{0,8},{4,12},{8,0},{12,4},{16,24},{20,28},{24,16},{28,20},{1,9},{5... | collective-permute-start | bytes 786440 | tf_op jit(solution)/shard_map/ppermute | solution.py:221
  11.3 0.5 %collective-permute-start.2 = (bf16[1024,128]{1,0:T(8,128)(2,1)S(1)}, bf16[1024,128]{1,0:T(8,128)(2,1)S(1)}, u32[]{:S(2)}, u32[]{:S(2)}) collective-permute-start(bf16[1024,128]{1,0:T(8,128)(2,1)S(1)} %shard_map.47), channel_id=1, source_target_pairs={{0,16},{4,20},{8,24},{12,28},{16,0},{20,4},{24,8},{28,12},{1,17},{... | collective-permute-start | bytes 786440 | tf_op jit(solution)/shard_map/ppermute | solution.py:221
  11.8 0.9 %collective-permute-done.3.theirs_ref = bf16[1024,128]{1,0:T(8,128)(2,1)S(1)} collective-permute-done((bf16[1024,128]{1,0:T(8,128)(2,1)}, bf16[1024,128]{1,0:T(8,128)(2,1)S(1)}, u32[]{:S(2)}, u32[]{:S(2)}) %collective-permute-start.3) | collective-permute-done | bytes 262176 | tf_op jit(solution)/shard_map/ppermute | solution.py:221
  12.7 1.6 %shard_map.50 = (f32[272,256]{1,0:T(8,128)S(1)}, f32[272,256]{1,0:T(8,128)S(1)}, bf16[544,256]{1,0:T(8,128)(2,1)S(1)}) custom-call(bf16[1024,128]{1,0:T(8,128)(2,1)S(1)} %collective-permute-done.3.theirs_ref, bf16[1088,2304]{1,0:T(8,128)(2,1)S(1)} %shard_map.48.lhs_ref), custom_call_target="tpu_custom_call" | custom-call | flops 6000000000 | bytes 18000000 | tf_op jit(solution)/shard_map/pallas_call | solution.py:311
  14.3 2.5 %collective-permute-start.10 = (bf16[544,256]{1,0:T(8,128)(2,1)S(1)}, bf16[544,256]{1,0:T(8,128)(2,1)S(1)}, u32[]{:S(2)}, u32[]{:S(2)}) collective-permute-start(bf16[544,256]{1,0:T(8,128)(2,1)S(1)} %get-tuple-element.17), channel_id=1, source_target_pairs={{0,1},{1,0},{2,3},{3,2},{4,5},{5,4},{6,7},{7,6},{8,9},{9,8},{10,11... | collective-permute-start | bytes 835592 | tf_op jit(solution)/shard_map/ppermute | solution.py:221
  16.8 0.0 collective-permute-done.6.white_ref
  16.8 0.0 collective-permute-start.7
  16.8 0.5 %collective-permute-start.4 = (bf16[1024,128]{1,0:T(8,128)(2,1)S(1)}, bf16[1024,128]{1,0:T(8,128)(2,1)S(1)}, u32[]{:S(2)}, u32[]{:S(2)}) collective-permute-start(bf16[1024,128]{1,0:T(8,128)(2,1)S(1)} %collective-permute-done.3.theirs_ref), channel_id=1, source_target_pairs={{0,4},{4,0},{8,12},{12,8},{16,20},{20,16},{24,28},{28,24},{1,5},{5... | collective-permute-start | bytes 786440 | tf_op jit(solution)/shard_map/ppermute | solution.py:221
  17.3 0.8 %shard_map.51.lhs2_ref = bf16[544,2304]{1,0:T(8,128)(2,1)S(1)} custom-call(bf16[1024,128]{1,0:T(8,128)(2,1)S(1)} %collective-permute-done.6.white_ref), custom_call_target="tpu_custom_call" | custom-call | flops 4499999744 | bytes 13500000 | tf_op jit(solution)/shard_map/pallas_call | solution.py:253
  18.1 1.1 %collective-permute-done.1.x_ref = bf16[1024,128]{1,0:T(8,128)(2,1)S(1)} collective-permute-done((bf16[1024,128]{1,0:T(8,128)(2,1)S(1)}, bf16[1024,128]{1,0:T(8,128)(2,1)S(1)}, u32[]{:S(2)}, u32[]{:S(2)}) %collective-permute-start.1) | collective-permute-done | bytes 262176 | tf_op jit(solution)/shard_map/ppermute | solution.py:221
  19.2 0.1 collective-permute-done.2.y_ref
  19.3 0.0 collective-permute-done.4.corner_ref
  19.3 1.8 %shard_map.49 = (f32[272,256]{1,0:T(8,128)S(1)}, f32[272,256]{1,0:T(8,128)S(1)}, bf16[544,256]{1,0:T(8,128)(2,1)S(1)}) custom-call(s32[1,3]{1,0:T(1,128)S(1)} %bitcast.2, bf16[1024,128]{1,0:T(8,128)(2,1)S(1)} %collective-permute-done.1.x_ref, bf16[1024,128]{1,0:T(8,128)(2,1)S(1)} %collective-permute-done.2.y_ref, ...), custom_call_target="tpu_custom_call" | custom-call | flops 6000000000 | bytes 18000000 | tf_op jit(solution)/shard_map/pallas_call | solution.py:313
  21.1 1.6 %collective-permute-start.5 = (bf16[544,256]{1,0:T(8,128)(2,1)S(1)}, bf16[544,256]{1,0:T(8,128)(2,1)S(1)}, u32[]{:S(2)}, u32[]{:S(2)}) collective-permute-start(bf16[544,256]{1,0:T(8,128)(2,1)S(1)} %get-tuple-element.16), channel_id=1, source_target_pairs={{0,1},{1,0},{2,3},{3,2},{4,5},{5,4},{6,7},{7,6},{8,9},{9,8},{10,11... | collective-permute-start | bytes 835592 | tf_op jit(solution)/shard_map/ppermute | solution.py:221
  22.7 1.7 %shard_map.52 = (f32[272,256]{1,0:T(8,128)S(1)}, bf16[272,256]{1,0:T(8,128)(2,1)S(1)}) custom-call(bf16[1024,128]{1,0:T(8,128)(2,1)S(1)} %collective-permute-done.near_ref.theirs_ref, bf16[1088,2304]{1,0:T(8,128)(2,1)S(1)} %shard_map.48.lhs_ref, bf16[1024,128]{1,0:T(8,128)(2,1)S(1)} %collective-permute-done.7.theirs2_ref, ...), custom_call_target="tpu_custom_call" | custom-call | flops 6000000000 | bytes 18000000 | tf_op jit(solution)/shard_map/pallas_call | solution.py:336
  24.4 2.7 %collective-permute-start.8 = (bf16[272,256]{1,0:T(8,128)(2,1)S(1)}, bf16[272,256]{1,0:T(8,128)(2,1)S(1)}, u32[]{:S(2)}, u32[]{:S(2)}) collective-permute-start(bf16[272,256]{1,0:T(8,128)(2,1)S(1)} %get-tuple-element.19), channel_id=1, source_target_pairs={{0,2},{1,3},{2,0},{3,1},{4,6},{5,7},{6,4},{7,5},{8,10},{9,11},{10,... | collective-permute-start | bytes 417800 | tf_op jit(solution)/shard_map/ppermute | solution.py:221
  27.1 0.4 collective-permute-start.11
  27.5 5.3 %collective-permute-done.8.refs_1_ = bf16[272,256]{1,0:T(8,128)(2,1)S(1)} collective-permute-done((bf16[272,256]{1,0:T(8,128)(2,1)S(1)}, bf16[272,256]{1,0:T(8,128)(2,1)S(1)}, u32[]{:S(2)}, u32[]{:S(2)}) %collective-permute-start.8) | collective-permute-done | bytes 139296 | tf_op jit(solution)/shard_map/ppermute | solution.py:221
  32.7 0.9 %collective-permute-done.5.refs_1_ = bf16[544,256]{1,0:T(8,128)(2,1)S(1)} collective-permute-done((bf16[544,256]{1,0:T(8,128)(2,1)S(1)}, bf16[544,256]{1,0:T(8,128)(2,1)S(1)}, u32[]{:S(2)}, u32[]{:S(2)}) %collective-permute-start.5) | collective-permute-done | bytes 278560 | tf_op jit(solution)/shard_map/ppermute | solution.py:221
  33.7 2.6 %collective-permute-start.9 = (bf16[272,256]{1,0:T(8,128)(2,1)S(1)}, bf16[272,256]{1,0:T(8,128)(2,1)S(1)}, u32[]{:S(2)}, u32[]{:S(2)}) collective-permute-start(bf16[272,256]{1,0:T(8,128)(2,1)S(1)} %add_convert_fusion.1), channel_id=1, source_target_pairs={{0,2},{1,3},{2,0},{3,1},{4,6},{5,7},{6,4},{7,5},{8,10},{9,11},{10,... | collective-permute-start | bytes 417800 | tf_op jit(solution)/shard_map/ppermute | solution.py:221
  36.3 5.5 %collective-permute-done.11.refs_4_ = bf16[272,256]{1,0:T(8,128)(2,1)S(1)} collective-permute-done((bf16[272,256]{1,0:T(8,128)(2,1)S(1)}, bf16[272,256]{1,0:T(8,128)(2,1)S(1)}, u32[]{:S(2)}, u32[]{:S(2)}) %collective-permute-start.11) | collective-permute-done | bytes 139296 | tf_op jit(solution)/shard_map/ppermute | solution.py:221
  41.8 1.5 %shard_map.53.refs_3_ = f32[3,65,1024]{2,1,0:T(8,128)} custom-call(s32[3]{0:T(128)S(1)} %copy-done.2, f32[272,256]{1,0:T(8,128)S(1)} %get-tuple-element.22.refs_0_, bf16[272,256]{1,0:T(8,128)(2,1)S(1)} %collective-permute-done.8.refs_1_, f32[272,256]{1,0:T(8,128)S(1)} %get-tuple-element.23.refs_2_, bf16[544,256]{1,0:T(8,128)(2,1)S(1)} %collective-permute-done.10.refs_3_, ...), custom_call_target="tpu_custom_call" | custom-call | flops 1000000000 | bytes 3000000 | tf_op jit(solution)/shard_map/pallas_call | solution.py:367
  43.3 0.9 %collective-permute-done.9.refs_2_ = bf16[272,256]{1,0:T(8,128)(2,1)S(1)} collective-permute-done((bf16[272,256]{1,0:T(8,128)(2,1)S(1)}, bf16[272,256]{1,0:T(8,128)(2,1)S(1)}, u32[]{:S(2)}, u32[]{:S(2)}) %collective-permute-start.9) | collective-permute-done | bytes 139296 | tf_op jit(solution)/shard_map/ppermute | solution.py:221
  44.2 1.4 %shard_map.54 = f32[3,65,1024]{2,1,0:T(8,128)} custom-call(s32[3]{0:T(128)S(1)} %copy-done.2, f32[272,256]{1,0:T(8,128)S(1)} %get-tuple-element.15.refs_0_, bf16[544,256]{1,0:T(8,128)(2,1)S(1)} %collective-permute-done.5.refs_1_, bf16[272,256]{1,0:T(8,128)(2,1)S(1)} %collective-permute-done.9.refs_2_, ...), custom_call_target="tpu_custom_call", output_to_operand_aliasing={{}: (4, {})} | custom-call | flops 1000000000 | bytes 3000000 | tf_op jit(solution)/shard_map/pallas_call | solution.py:367
  (9 shorter events, 0.1 us)
Async XLA Ops:
  0.0 10.1 %copy-start.2 = (s32[3]{0:T(128)S(1)}, s32[3]{0:T(128)}, u32[]{:S(2)}) copy-start(s32[3]{0:T(128)} %masks_hbm.3) | copy-start | bytes 40
  2.3 10.4 %collective-permute-start.3 = (bf16[1024,128]{1,0:T(8,128)(2,1)}, bf16[1024,128]{1,0:T(8,128)(2,1)S(1)}, u32[]{:S(2)}, u32[]{:S(2)}) collective-permute-start(bf16[1024,128]{1,0:T(8,128)(2,1)} %shard_map.46.white_ref), channel_id=1, source_target_pairs={{0,28},{4,24},{8,20},{12,16},{16,12},{20,8},{24,4},{28,0},{1,29},{... | collective-permute-start | bytes 786440 | tf_op jit(solution)/shard_map/ppermute | solution.py:221
  5.7 11.0 %collective-permute-start.6 = (bf16[1024,128]{1,0:T(8,128)(2,1)}, bf16[1024,128]{1,0:T(8,128)(2,1)S(1)}, u32[]{:S(2)}, u32[]{:S(2)}) collective-permute-start(bf16[1024,128]{1,0:T(8,128)(2,1)} %shard_map.46.white_ref), channel_id=1, source_target_pairs={{0,1},{1,0},{2,3},{3,2},{4,5},{5,4},{6,7},{7,6},{8,9},{9,8},{10,11... | collective-permute-start | bytes 786440 | tf_op jit(solution)/shard_map/ppermute | solution.py:221
  7.3 2.8 %collective-permute-start = (bf16[1024,128]{1,0:T(8,128)(2,1)}, bf16[1024,128]{1,0:T(8,128)(2,1)S(1)}, u32[]{:S(2)}, u32[]{:S(2)}) collective-permute-start(bf16[1024,128]{1,0:T(8,128)(2,1)} %shard_map.46.white_ref), channel_id=1, source_target_pairs={{0,4},{4,0},{8,12},{12,8},{16,20},{20,16},{24,28},{28,24},{1,5},{5... | collective-permute-start | bytes 786440 | tf_op jit(solution)/shard_map/ppermute | solution.py:221
  7.7 0.9 %copy-start = (bf16[1024,128]{1,0:T(8,128)(2,1)S(1)}, bf16[1024,128]{1,0:T(8,128)(2,1)}, u32[]{:S(2)}) copy-start(bf16[1024,128]{1,0:T(8,128)(2,1)} %shard_map.46.white_ref) | copy-start | bytes 786436
  8.6 1.5 %copy-start.1 = (bf16[1024,128]{1,0:T(8,128)(2,1)S(1)}, bf16[1024,128]{1,0:T(8,128)(2,1)}, u32[]{:S(2)}) copy-start(bf16[1024,128]{1,0:T(8,128)(2,1)} %shard_map.46.white_ref) | copy-start | bytes 786436
  10.7 8.5 %collective-permute-start.1 = (bf16[1024,128]{1,0:T(8,128)(2,1)S(1)}, bf16[1024,128]{1,0:T(8,128)(2,1)S(1)}, u32[]{:S(2)}, u32[]{:S(2)}) collective-permute-start(bf16[1024,128]{1,0:T(8,128)(2,1)S(1)} %shard_map.47), channel_id=1, source_target_pairs={{0,8},{4,12},{8,0},{12,4},{16,24},{20,28},{24,16},{28,20},{1,9},{5... | collective-permute-start | bytes 786440 | tf_op jit(solution)/shard_map/ppermute | solution.py:221
  11.3 8.1 %collective-permute-start.2 = (bf16[1024,128]{1,0:T(8,128)(2,1)S(1)}, bf16[1024,128]{1,0:T(8,128)(2,1)S(1)}, u32[]{:S(2)}, u32[]{:S(2)}) collective-permute-start(bf16[1024,128]{1,0:T(8,128)(2,1)S(1)} %shard_map.47), channel_id=1, source_target_pairs={{0,16},{4,20},{8,24},{12,28},{16,0},{20,4},{24,8},{28,12},{1,17},{... | collective-permute-start | bytes 786440 | tf_op jit(solution)/shard_map/ppermute | solution.py:221
  14.3 12.7 %collective-permute-start.10 = (bf16[544,256]{1,0:T(8,128)(2,1)S(1)}, bf16[544,256]{1,0:T(8,128)(2,1)S(1)}, u32[]{:S(2)}, u32[]{:S(2)}) collective-permute-start(bf16[544,256]{1,0:T(8,128)(2,1)S(1)} %get-tuple-element.17), channel_id=1, source_target_pairs={{0,1},{1,0},{2,3},{3,2},{4,5},{5,4},{6,7},{7,6},{8,9},{9,8},{10,11... | collective-permute-start | bytes 835592 | tf_op jit(solution)/shard_map/ppermute | solution.py:221
  16.8 5.9 %collective-permute-start.7 = (bf16[1024,128]{1,0:T(8,128)(2,1)S(1)}, bf16[1024,128]{1,0:T(8,128)(2,1)S(1)}, u32[]{:S(2)}, u32[]{:S(2)}) collective-permute-start(bf16[1024,128]{1,0:T(8,128)(2,1)S(1)} %collective-permute-done.6.white_ref), channel_id=1, source_target_pairs={{0,4},{4,0},{8,12},{12,8},{16,20},{20,16},{24,28},{28,24},{1,5},{5... | collective-permute-start | bytes 786440 | tf_op jit(solution)/shard_map/ppermute | solution.py:221
  16.8 2.6 %collective-permute-start.4 = (bf16[1024,128]{1,0:T(8,128)(2,1)S(1)}, bf16[1024,128]{1,0:T(8,128)(2,1)S(1)}, u32[]{:S(2)}, u32[]{:S(2)}) collective-permute-start(bf16[1024,128]{1,0:T(8,128)(2,1)S(1)} %collective-permute-done.3.theirs_ref), channel_id=1, source_target_pairs={{0,4},{4,0},{8,12},{12,8},{16,20},{20,16},{24,28},{28,24},{1,5},{5... | collective-permute-start | bytes 786440 | tf_op jit(solution)/shard_map/ppermute | solution.py:221
  21.1 12.6 %collective-permute-start.5 = (bf16[544,256]{1,0:T(8,128)(2,1)S(1)}, bf16[544,256]{1,0:T(8,128)(2,1)S(1)}, u32[]{:S(2)}, u32[]{:S(2)}) collective-permute-start(bf16[544,256]{1,0:T(8,128)(2,1)S(1)} %get-tuple-element.16), channel_id=1, source_target_pairs={{0,1},{1,0},{2,3},{3,2},{4,5},{5,4},{6,7},{7,6},{8,9},{9,8},{10,11... | collective-permute-start | bytes 835592 | tf_op jit(solution)/shard_map/ppermute | solution.py:221
  24.4 8.4 %collective-permute-start.8 = (bf16[272,256]{1,0:T(8,128)(2,1)S(1)}, bf16[272,256]{1,0:T(8,128)(2,1)S(1)}, u32[]{:S(2)}, u32[]{:S(2)}) collective-permute-start(bf16[272,256]{1,0:T(8,128)(2,1)S(1)} %get-tuple-element.19), channel_id=1, source_target_pairs={{0,2},{1,3},{2,0},{3,1},{4,6},{5,7},{6,4},{7,5},{8,10},{9,11},{10,... | collective-permute-start | bytes 417800 | tf_op jit(solution)/shard_map/ppermute | solution.py:221
  27.1 14.7 %collective-permute-start.11 = (bf16[272,256]{1,0:T(8,128)(2,1)S(1)}, bf16[272,256]{1,0:T(8,128)(2,1)S(1)}, u32[]{:S(2)}, u32[]{:S(2)}) collective-permute-start(bf16[272,256]{1,0:T(8,128)(2,1)S(1)} %add_convert_fusion), channel_id=1, source_target_pairs={{0,2},{1,3},{2,0},{3,1},{4,6},{5,7},{6,4},{7,5},{8,10},{9,11},{10,... | collective-permute-start | bytes 417800 | tf_op jit(solution)/shard_map/ppermute | solution.py:221
  33.7 10.5 %collective-permute-start.9 = (bf16[272,256]{1,0:T(8,128)(2,1)S(1)}, bf16[272,256]{1,0:T(8,128)(2,1)S(1)}, u32[]{:S(2)}, u32[]{:S(2)}) collective-permute-start(bf16[272,256]{1,0:T(8,128)(2,1)S(1)} %add_convert_fusion.1), channel_id=1, source_target_pairs={{0,2},{1,3},{2,0},{3,1},{4,6},{5,7},{6,4},{7,5},{8,10},{9,11},{10,... | collective-permute-start | bytes 417800 | tf_op jit(solution)/shard_map/ppermute | solution.py:221

commit v4 on v3

--- a/solution.py
+++ b/solution.py
@@ -165,15 +165,10 @@
 
 
 def passed_kernel(last, masks_ref, white_ref, near_ref, out_ref):
-    flip = other_core(third_mask(masks_ref, last))
-
-    @pl.when(flip)
-    def _():
-        out_ref[...] = near_ref[...]
-
-    @pl.when(jnp.logical_not(flip))
-    def _():
-        out_ref[...] = white_ref[...]
+    masks = masks_ref[...]
+    third = masks[:, 0:1] ^ masks[:, 1:2] ^ masks[:, 2:3] ^ 1 ^ last
+    white, near = white_ref[...].astype(jnp.float32), near_ref[...].astype(jnp.float32)
+    out_ref[...] = jnp.where(other_core(third), near, white).astype(jnp.bfloat16)
 
 
 def chosen_kernel(places, last, masks_ref, x_ref, y_ref, corner_ref, lhs_ref, *refs):
@@ -323,9 +318,9 @@
         passed = call(
             functools.partial(passed_kernel, last),
             jax.ShapeDtypeStruct(white.shape, bf16),
-            [SMEM] + [VMEM] * 2,
+            [VMEM] * 3,
             micros=0.5,
-        )(pair_masks, white, near)
+        )(pair_masks.reshape(1, -1), white, near)
         along_x = apart(passed, "chan", 2)
         along_y = apart(passed, "chan", 4)
     far_done, far_sum = day_sum(FAR, far)

time: 46 us -> 45.9 us (level)
  transfers between devices with their start and end apart: 12 -> 12, of which waited for: 7 -> 6; matrix products, arithmetic and copies ran while one was open for 0% -> 0% of each run, Pallas kernels for 20% -> 20%
where the time goes in v4:
time: 45.9 us; the launch traced here: 45.7 us
  starting transfers between devices  16.8 us (37%)
  waiting for transfers between devices  15 us (33%)
  Pallas kernels  12.7 us (28%)
  local copies, waits for them, and re-layouts  0.96 us (2%)
    ppermute x12, starting transfers between devices, apart(): lax.ppermute(value, axis, [(s, s ^ mask) for s in range(lax.axis_size(axi...  16.8 us
    ppermute x12, waiting for transfers between devices, apart(): lax.ppermute(value, axis, [(s, s ^ mask) for s in range(lax.axis_size(axi...  15 us
    pallas_call x2, Pallas kernels, finish(): pl.pallas_call(functools.partial(finish_kernel, share, norm, last, names,...  2.89 us
    pallas_call x1, Pallas kernels, local(): call(whiten_kernel, jax.ShapeDtypeStruct((L, 2 * chans), bf16), [HBM] * 3...  2.31 us
    pallas_call x2, Pallas kernels, prepare(): call(functools.partial(prepare_kernel, days, count), jax.ShapeDtypeStruct...  2.23 us
    pallas_call x1, Pallas kernels, day_sum(): call(functools.partial(chosen_kernel, places, last), shapes, [VMEM] * (le...  1.76 us
    pallas_call x1, Pallas kernels, local(): call(paired_kernel, [jax.ShapeDtypeStruct((slot_rows, 256), f32), jax.Sha...  1.73 us
    pallas_call x1, Pallas kernels, day_sum(): call(functools.partial(known_kernel, places), shapes, [VMEM] * 2, [weight...  1.58 us
  transfers between devices with their start and end apart: 12, of which 6 were waited for; matrix products, arithmetic and copies ran while one was open for 0% of the time, Pallas kernels for 20%

profile of v4, /device:TPU:0, one launch (start us, length us, event | category | flops | bytes accessed | tf_op | source)
XLA Modules:
  0.0 45.7 jit_solution(14600155589437654322)
XLA Ops:
  0.0 2.3 %shard_map.46.white_ref = bf16[1024,128]{1,0:T(8,128)(2,1)} custom-call(s32[1,2]{1,0:T(1,128)} %off_hbm.1, bf16[1,64]{1,0:T(2,128)(2,1)} %bitcast.4, bf16[1,64,4096]{2,1,0:T(8,128)(2,1)} %rec_hbm.1), custom_call_target="tpu_custom_call" | custom-call | flops 6000000000 | bytes 18000000 | tf_op jit(solution)/shard_map/pallas_call | solution.py:227
  2.3 3.4 %collective-permute-start.3 = (bf16[1024,128]{1,0:T(8,128)(2,1)}, bf16[1024,128]{1,0:T(8,128)(2,1)S(1)}, u32[]{:S(2)}, u32[]{:S(2)}) collective-permute-start(bf16[1024,128]{1,0:T(8,128)(2,1)} %shard_map.46.white_ref), channel_id=1, source_target_pairs={{0,28},{4,24},{8,20},{12,16},{16,12},{20,8},{24,4},{28,0},{1,29},{... | collective-permute-start | bytes 786440 | tf_op jit(solution)/shard_map/ppermute | solution.py:216
  5.7 1.6 %collective-permute-start.6 = (bf16[1024,128]{1,0:T(8,128)(2,1)}, bf16[1024,128]{1,0:T(8,128)(2,1)S(1)}, u32[]{:S(2)}, u32[]{:S(2)}) collective-permute-start(bf16[1024,128]{1,0:T(8,128)(2,1)} %shard_map.46.white_ref), channel_id=1, source_target_pairs={{0,1},{1,0},{2,3},{3,2},{4,5},{5,4},{6,7},{7,6},{8,9},{9,8},{10,11... | collective-permute-start | bytes 786440 | tf_op jit(solution)/shard_map/ppermute | solution.py:216
  7.3 0.4 collective-permute-start
  7.7 0.9 %copy-done = bf16[1024,128]{1,0:T(8,128)(2,1)S(1)} copy-done((bf16[1024,128]{1,0:T(8,128)(2,1)S(1)}, bf16[1024,128]{1,0:T(8,128)(2,1)}, u32[]{:S(2)}) %copy-start) | copy-done | bytes 262168
  8.7 1.4 %shard_map.48.lhs_ref = bf16[1088,2304]{1,0:T(8,128)(2,1)S(1)} custom-call(bf16[1024,128]{1,0:T(8,128)(2,1)S(1)} %copy-done), custom_call_target="tpu_custom_call" | custom-call | flops 4499999744 | bytes 13500000 | tf_op jit(solution)/shard_map/pallas_call | solution.py:248
  10.1 0.0 collective-permute-done.near_ref.theirs_ref
  10.1 0.2 shard_map.47
  10.3 0.6 %collective-permute-start.1 = (bf16[1024,128]{1,0:T(8,128)(2,1)S(1)}, bf16[1024,128]{1,0:T(8,128)(2,1)S(1)}, u32[]{:S(2)}, u32[]{:S(2)}) collective-permute-start(bf16[1024,128]{1,0:T(8,128)(2,1)S(1)} %shard_map.47), channel_id=1, source_target_pairs={{0,8},{4,12},{8,0},{12,4},{16,24},{20,28},{24,16},{28,20},{1,9},{5... | collective-permute-start | bytes 786440 | tf_op jit(solution)/shard_map/ppermute | solution.py:216
  10.9 0.5 %collective-permute-start.2 = (bf16[1024,128]{1,0:T(8,128)(2,1)S(1)}, bf16[1024,128]{1,0:T(8,128)(2,1)S(1)}, u32[]{:S(2)}, u32[]{:S(2)}) collective-permute-start(bf16[1024,128]{1,0:T(8,128)(2,1)S(1)} %shard_map.47), channel_id=1, source_target_pairs={{0,16},{4,20},{8,24},{12,28},{16,0},{20,4},{24,8},{28,12},{1,17},{... | collective-permute-start | bytes 786440 | tf_op jit(solution)/shard_map/ppermute | solution.py:216
  11.4 1.3 %collective-permute-done.3.theirs_ref = bf16[1024,128]{1,0:T(8,128)(2,1)S(1)} collective-permute-done((bf16[1024,128]{1,0:T(8,128)(2,1)}, bf16[1024,128]{1,0:T(8,128)(2,1)S(1)}, u32[]{:S(2)}, u32[]{:S(2)}) %collective-permute-start.3) | collective-permute-done | bytes 262176 | tf_op jit(solution)/shard_map/ppermute | solution.py:216
  12.7 1.6 %shard_map.50 = (f32[272,256]{1,0:T(8,128)S(1)}, f32[272,256]{1,0:T(8,128)S(1)}, bf16[544,256]{1,0:T(8,128)(2,1)S(1)}) custom-call(bf16[1024,128]{1,0:T(8,128)(2,1)S(1)} %collective-permute-done.3.theirs_ref, bf16[1088,2304]{1,0:T(8,128)(2,1)S(1)} %shard_map.48.lhs_ref), custom_call_target="tpu_custom_call" | custom-call | flops 6000000000 | bytes 18000000 | tf_op jit(solution)/shard_map/pallas_call | solution.py:306
  14.3 2.5 %collective-permute-start.10 = (bf16[544,256]{1,0:T(8,128)(2,1)S(1)}, bf16[544,256]{1,0:T(8,128)(2,1)S(1)}, u32[]{:S(2)}, u32[]{:S(2)}) collective-permute-start(bf16[544,256]{1,0:T(8,128)(2,1)S(1)} %get-tuple-element.17), channel_id=1, source_target_pairs={{0,1},{1,0},{2,3},{3,2},{4,5},{5,4},{6,7},{7,6},{8,9},{9,8},{10,11... | collective-permute-start | bytes 835592 | tf_op jit(solution)/shard_map/ppermute | solution.py:216
  16.8 0.0 collective-permute-done.6.white_ref
  16.8 0.0 collective-permute-start.7
  16.8 0.5 %collective-permute-start.4 = (bf16[1024,128]{1,0:T(8,128)(2,1)S(1)}, bf16[1024,128]{1,0:T(8,128)(2,1)S(1)}, u32[]{:S(2)}, u32[]{:S(2)}) collective-permute-start(bf16[1024,128]{1,0:T(8,128)(2,1)S(1)} %collective-permute-done.3.theirs_ref), channel_id=1, source_target_pairs={{0,4},{4,0},{8,12},{12,8},{16,20},{20,16},{24,28},{28,24},{1,5},{5... | collective-permute-start | bytes 786440 | tf_op jit(solution)/shard_map/ppermute | solution.py:216
  17.3 0.8 %shard_map.51.lhs2_ref = bf16[544,2304]{1,0:T(8,128)(2,1)S(1)} custom-call(bf16[1024,128]{1,0:T(8,128)(2,1)S(1)} %collective-permute-done.6.white_ref), custom_call_target="tpu_custom_call" | custom-call | flops 4499999744 | bytes 13500000 | tf_op jit(solution)/shard_map/pallas_call | solution.py:248
  18.1 1.1 %collective-permute-done.1.x_ref = bf16[1024,128]{1,0:T(8,128)(2,1)S(1)} collective-permute-done((bf16[1024,128]{1,0:T(8,128)(2,1)S(1)}, bf16[1024,128]{1,0:T(8,128)(2,1)S(1)}, u32[]{:S(2)}, u32[]{:S(2)}) %collective-permute-start.1) | collective-permute-done | bytes 262176 | tf_op jit(solution)/shard_map/ppermute | solution.py:216
  19.2 0.0 collective-permute-done.2.y_ref
  19.2 0.0 collective-permute-done.4.corner_ref
  19.2 1.8 %shard_map.49 = (f32[272,256]{1,0:T(8,128)S(1)}, f32[272,256]{1,0:T(8,128)S(1)}, bf16[544,256]{1,0:T(8,128)(2,1)S(1)}) custom-call(s32[1,3]{1,0:T(1,128)S(1)} %bitcast.3, bf16[1024,128]{1,0:T(8,128)(2,1)S(1)} %collective-permute-done.1.x_ref, bf16[1024,128]{1,0:T(8,128)(2,1)S(1)} %collective-permute-done.2.y_ref, ...), custom_call_target="tpu_custom_call" | custom-call | flops 6000000000 | bytes 18000000 | tf_op jit(solution)/shard_map/pallas_call | solution.py:308
  21.0 1.7 %collective-permute-start.5 = (bf16[544,256]{1,0:T(8,128)(2,1)S(1)}, bf16[544,256]{1,0:T(8,128)(2,1)S(1)}, u32[]{:S(2)}, u32[]{:S(2)}) collective-permute-start(bf16[544,256]{1,0:T(8,128)(2,1)S(1)} %get-tuple-element.16), channel_id=1, source_target_pairs={{0,1},{1,0},{2,3},{3,2},{4,5},{5,4},{6,7},{7,6},{8,9},{9,8},{10,11... | collective-permute-start | bytes 835592 | tf_op jit(solution)/shard_map/ppermute | solution.py:216
  22.7 1.7 %shard_map.52 = (f32[272,256]{1,0:T(8,128)S(1)}, bf16[272,256]{1,0:T(8,128)(2,1)S(1)}) custom-call(bf16[1024,128]{1,0:T(8,128)(2,1)S(1)} %collective-permute-done.near_ref.theirs_ref, bf16[1088,2304]{1,0:T(8,128)(2,1)S(1)} %shard_map.48.lhs_ref, bf16[1024,128]{1,0:T(8,128)(2,1)S(1)} %collective-permute-done.7.theirs2_ref, ...), custom_call_target="tpu_custom_call" | custom-call | flops 6000000000 | bytes 18000000 | tf_op jit(solution)/shard_map/pallas_call | solution.py:331
  24.4 2.7 %collective-permute-start.8 = (bf16[272,256]{1,0:T(8,128)(2,1)S(1)}, bf16[272,256]{1,0:T(8,128)(2,1)S(1)}, u32[]{:S(2)}, u32[]{:S(2)}) collective-permute-start(bf16[272,256]{1,0:T(8,128)(2,1)S(1)} %get-tuple-element.19), channel_id=1, source_target_pairs={{0,2},{1,3},{2,0},{3,1},{4,6},{5,7},{6,4},{7,5},{8,10},{9,11},{10,... | collective-permute-start | bytes 417800 | tf_op jit(solution)/shard_map/ppermute | solution.py:216
  27.1 0.4 collective-permute-start.11
  27.5 5.2 %collective-permute-done.8.refs_1_ = bf16[272,256]{1,0:T(8,128)(2,1)S(1)} collective-permute-done((bf16[272,256]{1,0:T(8,128)(2,1)S(1)}, bf16[272,256]{1,0:T(8,128)(2,1)S(1)}, u32[]{:S(2)}, u32[]{:S(2)}) %collective-permute-start.8) | collective-permute-done | bytes 139296 | tf_op jit(solution)/shard_map/ppermute | solution.py:216
  32.7 0.9 %collective-permute-done.5.refs_1_ = bf16[544,256]{1,0:T(8,128)(2,1)S(1)} collective-permute-done((bf16[544,256]{1,0:T(8,128)(2,1)S(1)}, bf16[544,256]{1,0:T(8,128)(2,1)S(1)}, u32[]{:S(2)}, u32[]{:S(2)}) %collective-permute-start.5) | collective-permute-done | bytes 278560 | tf_op jit(solution)/shard_map/ppermute | solution.py:216
  33.7 2.6 %collective-permute-start.9 = (bf16[272,256]{1,0:T(8,128)(2,1)S(1)}, bf16[272,256]{1,0:T(8,128)(2,1)S(1)}, u32[]{:S(2)}, u32[]{:S(2)}) collective-permute-start(bf16[272,256]{1,0:T(8,128)(2,1)S(1)} %add_convert_fusion.1), channel_id=1, source_target_pairs={{0,2},{1,3},{2,0},{3,1},{4,6},{5,7},{6,4},{7,5},{8,10},{9,11},{10,... | collective-permute-start | bytes 417800 | tf_op jit(solution)/shard_map/ppermute | solution.py:216
  36.3 5.6 %collective-permute-done.11.refs_4_ = bf16[272,256]{1,0:T(8,128)(2,1)S(1)} collective-permute-done((bf16[272,256]{1,0:T(8,128)(2,1)S(1)}, bf16[272,256]{1,0:T(8,128)(2,1)S(1)}, u32[]{:S(2)}, u32[]{:S(2)}) %collective-permute-start.11) | collective-permute-done | bytes 139296 | tf_op jit(solution)/shard_map/ppermute | solution.py:216
  41.9 1.5 %shard_map.53.refs_3_ = f32[3,65,1024]{2,1,0:T(8,128)} custom-call(s32[3]{0:T(128)S(1)} %copy-done.2, f32[272,256]{1,0:T(8,128)S(1)} %get-tuple-element.22.refs_0_, bf16[272,256]{1,0:T(8,128)(2,1)S(1)} %collective-permute-done.8.refs_1_, f32[272,256]{1,0:T(8,128)S(1)} %get-tuple-element.23.refs_2_, bf16[544,256]{1,0:T(8,128)(2,1)S(1)} %collective-permute-done.10.refs_3_, ...), custom_call_target="tpu_custom_call" | custom-call | flops 1000000000 | bytes 3000000 | tf_op jit(solution)/shard_map/pallas_call | solution.py:362
  43.4 0.9 %collective-permute-done.9.refs_2_ = bf16[272,256]{1,0:T(8,128)(2,1)S(1)} collective-permute-done((bf16[272,256]{1,0:T(8,128)(2,1)S(1)}, bf16[272,256]{1,0:T(8,128)(2,1)S(1)}, u32[]{:S(2)}, u32[]{:S(2)}) %collective-permute-start.9) | collective-permute-done | bytes 139296 | tf_op jit(solution)/shard_map/ppermute | solution.py:216
  44.3 1.4 %shard_map.54 = f32[3,65,1024]{2,1,0:T(8,128)} custom-call(s32[3]{0:T(128)S(1)} %copy-done.2, f32[272,256]{1,0:T(8,128)S(1)} %get-tuple-element.15.refs_0_, bf16[544,256]{1,0:T(8,128)(2,1)S(1)} %collective-permute-done.5.refs_1_, bf16[272,256]{1,0:T(8,128)(2,1)S(1)} %collective-permute-done.9.refs_2_, ...), custom_call_target="tpu_custom_call", output_to_operand_aliasing={{}: (4, {})} | custom-call | flops 1000000000 | bytes 3000000 | tf_op jit(solution)/shard_map/pallas_call | solution.py:362
  (9 shorter events, 0.1 us)
Async XLA Ops:
  0.0 10.1 %copy-start.2 = (s32[3]{0:T(128)S(1)}, s32[3]{0:T(128)}, u32[]{:S(2)}) copy-start(s32[3]{0:T(128)} %masks_hbm.3) | copy-start | bytes 40
  2.3 10.4 %collective-permute-start.3 = (bf16[1024,128]{1,0:T(8,128)(2,1)}, bf16[1024,128]{1,0:T(8,128)(2,1)S(1)}, u32[]{:S(2)}, u32[]{:S(2)}) collective-permute-start(bf16[1024,128]{1,0:T(8,128)(2,1)} %shard_map.46.white_ref), channel_id=1, source_target_pairs={{0,28},{4,24},{8,20},{12,16},{16,12},{20,8},{24,4},{28,0},{1,29},{... | collective-permute-start | bytes 786440 | tf_op jit(solution)/shard_map/ppermute | solution.py:216
  5.7 11.1 %collective-permute-start.6 = (bf16[1024,128]{1,0:T(8,128)(2,1)}, bf16[1024,128]{1,0:T(8,128)(2,1)S(1)}, u32[]{:S(2)}, u32[]{:S(2)}) collective-permute-start(bf16[1024,128]{1,0:T(8,128)(2,1)} %shard_map.46.white_ref), channel_id=1, source_target_pairs={{0,1},{1,0},{2,3},{3,2},{4,5},{5,4},{6,7},{7,6},{8,9},{9,8},{10,11... | collective-permute-start | bytes 786440 | tf_op jit(solution)/shard_map/ppermute | solution.py:216
  7.3 2.8 %collective-permute-start = (bf16[1024,128]{1,0:T(8,128)(2,1)}, bf16[1024,128]{1,0:T(8,128)(2,1)S(1)}, u32[]{:S(2)}, u32[]{:S(2)}) collective-permute-start(bf16[1024,128]{1,0:T(8,128)(2,1)} %shard_map.46.white_ref), channel_id=1, source_target_pairs={{0,4},{4,0},{8,12},{12,8},{16,20},{20,16},{24,28},{28,24},{1,5},{5... | collective-permute-start | bytes 786440 | tf_op jit(solution)/shard_map/ppermute | solution.py:216
  7.7 0.9 %copy-start = (bf16[1024,128]{1,0:T(8,128)(2,1)S(1)}, bf16[1024,128]{1,0:T(8,128)(2,1)}, u32[]{:S(2)}) copy-start(bf16[1024,128]{1,0:T(8,128)(2,1)} %shard_map.46.white_ref) | copy-start | bytes 786436
  8.6 1.5 %copy-start.1 = (bf16[1024,128]{1,0:T(8,128)(2,1)S(1)}, bf16[1024,128]{1,0:T(8,128)(2,1)}, u32[]{:S(2)}) copy-start(bf16[1024,128]{1,0:T(8,128)(2,1)} %shard_map.46.white_ref) | copy-start | bytes 786436
  10.3 8.9 %collective-permute-start.1 = (bf16[1024,128]{1,0:T(8,128)(2,1)S(1)}, bf16[1024,128]{1,0:T(8,128)(2,1)S(1)}, u32[]{:S(2)}, u32[]{:S(2)}) collective-permute-start(bf16[1024,128]{1,0:T(8,128)(2,1)S(1)} %shard_map.47), channel_id=1, source_target_pairs={{0,8},{4,12},{8,0},{12,4},{16,24},{20,28},{24,16},{28,20},{1,9},{5... | collective-permute-start | bytes 786440 | tf_op jit(solution)/shard_map/ppermute | solution.py:216
  10.9 8.3 %collective-permute-start.2 = (bf16[1024,128]{1,0:T(8,128)(2,1)S(1)}, bf16[1024,128]{1,0:T(8,128)(2,1)S(1)}, u32[]{:S(2)}, u32[]{:S(2)}) collective-permute-start(bf16[1024,128]{1,0:T(8,128)(2,1)S(1)} %shard_map.47), channel_id=1, source_target_pairs={{0,16},{4,20},{8,24},{12,28},{16,0},{20,4},{24,8},{28,12},{1,17},{... | collective-permute-start | bytes 786440 | tf_op jit(solution)/shard_map/ppermute | solution.py:216
  14.3 12.8 %collective-permute-start.10 = (bf16[544,256]{1,0:T(8,128)(2,1)S(1)}, bf16[544,256]{1,0:T(8,128)(2,1)S(1)}, u32[]{:S(2)}, u32[]{:S(2)}) collective-permute-start(bf16[544,256]{1,0:T(8,128)(2,1)S(1)} %get-tuple-element.17), channel_id=1, source_target_pairs={{0,1},{1,0},{2,3},{3,2},{4,5},{5,4},{6,7},{7,6},{8,9},{9,8},{10,11... | collective-permute-start | bytes 835592 | tf_op jit(solution)/shard_map/ppermute | solution.py:216
  16.8 5.9 %collective-permute-start.7 = (bf16[1024,128]{1,0:T(8,128)(2,1)S(1)}, bf16[1024,128]{1,0:T(8,128)(2,1)S(1)}, u32[]{:S(2)}, u32[]{:S(2)}) collective-permute-start(bf16[1024,128]{1,0:T(8,128)(2,1)S(1)} %collective-permute-done.6.white_ref), channel_id=1, source_target_pairs={{0,4},{4,0},{8,12},{12,8},{16,20},{20,16},{24,28},{28,24},{1,5},{5... | collective-permute-start | bytes 786440 | tf_op jit(solution)/shard_map/ppermute | solution.py:216
  16.8 2.4 %collective-permute-start.4 = (bf16[1024,128]{1,0:T(8,128)(2,1)S(1)}, bf16[1024,128]{1,0:T(8,128)(2,1)S(1)}, u32[]{:S(2)}, u32[]{:S(2)}) collective-permute-start(bf16[1024,128]{1,0:T(8,128)(2,1)S(1)} %collective-permute-done.3.theirs_ref), channel_id=1, source_target_pairs={{0,4},{4,0},{8,12},{12,8},{16,20},{20,16},{24,28},{28,24},{1,5},{5... | collective-permute-start | bytes 786440 | tf_op jit(solution)/shard_map/ppermute | solution.py:216
  21.0 12.7 %collective-permute-start.5 = (bf16[544,256]{1,0:T(8,128)(2,1)S(1)}, bf16[544,256]{1,0:T(8,128)(2,1)S(1)}, u32[]{:S(2)}, u32[]{:S(2)}) collective-permute-start(bf16[544,256]{1,0:T(8,128)(2,1)S(1)} %get-tuple-element.16), channel_id=1, source_target_pairs={{0,1},{1,0},{2,3},{3,2},{4,5},{5,4},{6,7},{7,6},{8,9},{9,8},{10,11... | collective-permute-start | bytes 835592 | tf_op jit(solution)/shard_map/ppermute | solution.py:216
  24.4 8.3 %collective-permute-start.8 = (bf16[272,256]{1,0:T(8,128)(2,1)S(1)}, bf16[272,256]{1,0:T(8,128)(2,1)S(1)}, u32[]{:S(2)}, u32[]{:S(2)}) collective-permute-start(bf16[272,256]{1,0:T(8,128)(2,1)S(1)} %get-tuple-element.19), channel_id=1, source_target_pairs={{0,2},{1,3},{2,0},{3,1},{4,6},{5,7},{6,4},{7,5},{8,10},{9,11},{10,... | collective-permute-start | bytes 417800 | tf_op jit(solution)/shard_map/ppermute | solution.py:216
  27.1 14.7 %collective-permute-start.11 = (bf16[272,256]{1,0:T(8,128)(2,1)S(1)}, bf16[272,256]{1,0:T(8,128)(2,1)S(1)}, u32[]{:S(2)}, u32[]{:S(2)}) collective-permute-start(bf16[272,256]{1,0:T(8,128)(2,1)S(1)} %add_convert_fusion), channel_id=1, source_target_pairs={{0,2},{1,3},{2,0},{3,1},{4,6},{5,7},{6,4},{7,5},{8,10},{9,11},{10,... | collective-permute-start | bytes 417800 | tf_op jit(solution)/shard_map/ppermute | solution.py:216
  33.7 10.6 %collective-permute-start.9 = (bf16[272,256]{1,0:T(8,128)(2,1)S(1)}, bf16[272,256]{1,0:T(8,128)(2,1)S(1)}, u32[]{:S(2)}, u32[]{:S(2)}) collective-permute-start(bf16[272,256]{1,0:T(8,128)(2,1)S(1)} %add_convert_fusion.1), channel_id=1, source_target_pairs={{0,2},{1,3},{2,0},{3,1},{4,6},{5,7},{6,4},{7,5},{8,10},{9,11},{10,... | collective-permute-start | bytes 417800 | tf_op jit(solution)/shard_map/ppermute | solution.py:216

commit v5 on v4

--- a/solution.py
+++ b/solution.py
@@ -15,7 +15,7 @@
 PLANES = FINE + 1
 PAD = 1152
 CUT = 1280
-COST = 3.0
+COST = 2.5
 DIRECT_ORDER = (2, 3, 1)
 FAR_AFTER = False
 LAST_AFTER = 1

time: 45.9 us -> 45.9 us (level)
  no operation moved by 1% of the time
where the time goes in v5:
time: 45.9 us; the launch traced here: 45.7 us
  starting transfers between devices  16.8 us (37%)
  waiting for transfers between devices  15 us (33%)
  Pallas kernels  12.7 us (28%)
  local copies, waits for them, and re-layouts  0.96 us (2%)
    ppermute x12, starting transfers between devices, apart(): lax.ppermute(value, axis, [(s, s ^ mask) for s in range(lax.axis_size(axi...  16.8 us
    ppermute x12, waiting for transfers between devices, apart(): lax.ppermute(value, axis, [(s, s ^ mask) for s in range(lax.axis_size(axi...  15 us
    pallas_call x2, Pallas kernels, finish(): pl.pallas_call(functools.partial(finish_kernel, share, norm, last, names,...  2.89 us
    pallas_call x1, Pallas kernels, local(): call(whiten_kernel, jax.ShapeDtypeStruct((L, 2 * chans), bf16), [HBM] * 3...  2.31 us
    pallas_call x2, Pallas kernels, prepare(): call(functools.partial(prepare_kernel, days, count), jax.ShapeDtypeStruct...  2.23 us
    pallas_call x1, Pallas kernels, day_sum(): call(functools.partial(chosen_kernel, places, last), shapes, [VMEM] * (le...  1.76 us
    pallas_call x1, Pallas kernels, local(): call(paired_kernel, [jax.ShapeDtypeStruct((slot_rows, 256), f32), jax.Sha...  1.73 us
    pallas_call x1, Pallas kernels, day_sum(): call(functools.partial(known_kernel, places), shapes, [VMEM] * 2, [weight...  1.58 us
  transfers between devices with their start and end apart: 12, of which 6 were waited for; matrix products, arithmetic and copies ran while one was open for 0% of the time, Pallas kernels for 20%

profile of v5, /device:TPU:0, one launch (start us, length us, event | category | flops | bytes accessed | tf_op | source)
XLA Modules:
  0.0 45.7 jit_solution(14600155589437654322)
XLA Ops:
  0.0 2.3 %shard_map.46.white_ref = bf16[1024,128]{1,0:T(8,128)(2,1)} custom-call(s32[1,2]{1,0:T(1,128)} %off_hbm.1, bf16[1,64]{1,0:T(2,128)(2,1)} %bitcast.4, bf16[1,64,4096]{2,1,0:T(8,128)(2,1)} %rec_hbm.1), custom_call_target="tpu_custom_call" | custom-call | flops 5000000000 | bytes 15000000 | tf_op jit(solution)/shard_map/pallas_call | solution.py:227
  2.3 3.4 %collective-permute-start.3 = (bf16[1024,128]{1,0:T(8,128)(2,1)}, bf16[1024,128]{1,0:T(8,128)(2,1)S(1)}, u32[]{:S(2)}, u32[]{:S(2)}) collective-permute-start(bf16[1024,128]{1,0:T(8,128)(2,1)} %shard_map.46.white_ref), channel_id=1, source_target_pairs={{0,28},{4,24},{8,20},{12,16},{16,12},{20,8},{24,4},{28,0},{1,29},{... | collective-permute-start | bytes 786440 | tf_op jit(solution)/shard_map/ppermute | solution.py:216
  5.7 1.6 %collective-permute-start.6 = (bf16[1024,128]{1,0:T(8,128)(2,1)}, bf16[1024,128]{1,0:T(8,128)(2,1)S(1)}, u32[]{:S(2)}, u32[]{:S(2)}) collective-permute-start(bf16[1024,128]{1,0:T(8,128)(2,1)} %shard_map.46.white_ref), channel_id=1, source_target_pairs={{0,1},{1,0},{2,3},{3,2},{4,5},{5,4},{6,7},{7,6},{8,9},{9,8},{10,11... | collective-permute-start | bytes 786440 | tf_op jit(solution)/shard_map/ppermute | solution.py:216
  7.3 0.4 collective-permute-start
  7.7 0.9 %copy-done = bf16[1024,128]{1,0:T(8,128)(2,1)S(1)} copy-done((bf16[1024,128]{1,0:T(8,128)(2,1)S(1)}, bf16[1024,128]{1,0:T(8,128)(2,1)}, u32[]{:S(2)}) %copy-start) | copy-done | bytes 262168
  8.7 1.4 %shard_map.48.lhs_ref = bf16[1088,2304]{1,0:T(8,128)(2,1)S(1)} custom-call(bf16[1024,128]{1,0:T(8,128)(2,1)S(1)} %copy-done), custom_call_target="tpu_custom_call" | custom-call | flops 3750000128 | bytes 11250000 | tf_op jit(solution)/shard_map/pallas_call | solution.py:248
  10.1 0.0 collective-permute-done.near_ref.theirs_ref
  10.1 0.2 shard_map.47
  10.3 0.6 %collective-permute-start.1 = (bf16[1024,128]{1,0:T(8,128)(2,1)S(1)}, bf16[1024,128]{1,0:T(8,128)(2,1)S(1)}, u32[]{:S(2)}, u32[]{:S(2)}) collective-permute-start(bf16[1024,128]{1,0:T(8,128)(2,1)S(1)} %shard_map.47), channel_id=1, source_target_pairs={{0,8},{4,12},{8,0},{12,4},{16,24},{20,28},{24,16},{28,20},{1,9},{5... | collective-permute-start | bytes 786440 | tf_op jit(solution)/shard_map/ppermute | solution.py:216
  10.9 0.5 %collective-permute-start.2 = (bf16[1024,128]{1,0:T(8,128)(2,1)S(1)}, bf16[1024,128]{1,0:T(8,128)(2,1)S(1)}, u32[]{:S(2)}, u32[]{:S(2)}) collective-permute-start(bf16[1024,128]{1,0:T(8,128)(2,1)S(1)} %shard_map.47), channel_id=1, source_target_pairs={{0,16},{4,20},{8,24},{12,28},{16,0},{20,4},{24,8},{28,12},{1,17},{... | collective-permute-start | bytes 786440 | tf_op jit(solution)/shard_map/ppermute | solution.py:216
  11.4 1.3 %collective-permute-done.3.theirs_ref = bf16[1024,128]{1,0:T(8,128)(2,1)S(1)} collective-permute-done((bf16[1024,128]{1,0:T(8,128)(2,1)}, bf16[1024,128]{1,0:T(8,128)(2,1)S(1)}, u32[]{:S(2)}, u32[]{:S(2)}) %collective-permute-start.3) | collective-permute-done | bytes 262176 | tf_op jit(solution)/shard_map/ppermute | solution.py:216
  12.7 1.6 %shard_map.50 = (f32[272,256]{1,0:T(8,128)S(1)}, f32[272,256]{1,0:T(8,128)S(1)}, bf16[544,256]{1,0:T(8,128)(2,1)S(1)}) custom-call(bf16[1024,128]{1,0:T(8,128)(2,1)S(1)} %collective-permute-done.3.theirs_ref, bf16[1088,2304]{1,0:T(8,128)(2,1)S(1)} %shard_map.48.lhs_ref), custom_call_target="tpu_custom_call" | custom-call | flops 5000000000 | bytes 15000000 | tf_op jit(solution)/shard_map/pallas_call | solution.py:306
  14.3 2.5 %collective-permute-start.10 = (bf16[544,256]{1,0:T(8,128)(2,1)S(1)}, bf16[544,256]{1,0:T(8,128)(2,1)S(1)}, u32[]{:S(2)}, u32[]{:S(2)}) collective-permute-start(bf16[544,256]{1,0:T(8,128)(2,1)S(1)} %get-tuple-element.17), channel_id=1, source_target_pairs={{0,1},{1,0},{2,3},{3,2},{4,5},{5,4},{6,7},{7,6},{8,9},{9,8},{10,11... | collective-permute-start | bytes 835592 | tf_op jit(solution)/shard_map/ppermute | solution.py:216
  16.8 0.0 collective-permute-done.6.white_ref
  16.8 0.0 collective-permute-start.7
  16.8 0.5 %collective-permute-start.4 = (bf16[1024,128]{1,0:T(8,128)(2,1)S(1)}, bf16[1024,128]{1,0:T(8,128)(2,1)S(1)}, u32[]{:S(2)}, u32[]{:S(2)}) collective-permute-start(bf16[1024,128]{1,0:T(8,128)(2,1)S(1)} %collective-permute-done.3.theirs_ref), channel_id=1, source_target_pairs={{0,4},{4,0},{8,12},{12,8},{16,20},{20,16},{24,28},{28,24},{1,5},{5... | collective-permute-start | bytes 786440 | tf_op jit(solution)/shard_map/ppermute | solution.py:216
  17.3 0.8 %shard_map.51.lhs2_ref = bf16[544,2304]{1,0:T(8,128)(2,1)S(1)} custom-call(bf16[1024,128]{1,0:T(8,128)(2,1)S(1)} %collective-permute-done.6.white_ref), custom_call_target="tpu_custom_call" | custom-call | flops 3750000128 | bytes 11250000 | tf_op jit(solution)/shard_map/pallas_call | solution.py:248
  18.1 1.1 %collective-permute-done.1.x_ref = bf16[1024,128]{1,0:T(8,128)(2,1)S(1)} collective-permute-done((bf16[1024,128]{1,0:T(8,128)(2,1)S(1)}, bf16[1024,128]{1,0:T(8,128)(2,1)S(1)}, u32[]{:S(2)}, u32[]{:S(2)}) %collective-permute-start.1) | collective-permute-done | bytes 262176 | tf_op jit(solution)/shard_map/ppermute | solution.py:216
  19.2 0.0 collective-permute-done.2.y_ref
  19.2 0.0 collective-permute-done.4.corner_ref
  19.2 1.8 %shard_map.49 = (f32[272,256]{1,0:T(8,128)S(1)}, f32[272,256]{1,0:T(8,128)S(1)}, bf16[544,256]{1,0:T(8,128)(2,1)S(1)}) custom-call(s32[1,3]{1,0:T(1,128)S(1)} %bitcast.3, bf16[1024,128]{1,0:T(8,128)(2,1)S(1)} %collective-permute-done.1.x_ref, bf16[1024,128]{1,0:T(8,128)(2,1)S(1)} %collective-permute-done.2.y_ref, ...), custom_call_target="tpu_custom_call" | custom-call | flops 5000000000 | bytes 15000000 | tf_op jit(solution)/shard_map/pallas_call | solution.py:308
  21.0 1.7 %collective-permute-start.5 = (bf16[544,256]{1,0:T(8,128)(2,1)S(1)}, bf16[544,256]{1,0:T(8,128)(2,1)S(1)}, u32[]{:S(2)}, u32[]{:S(2)}) collective-permute-start(bf16[544,256]{1,0:T(8,128)(2,1)S(1)} %get-tuple-element.16), channel_id=1, source_target_pairs={{0,1},{1,0},{2,3},{3,2},{4,5},{5,4},{6,7},{7,6},{8,9},{9,8},{10,11... | collective-permute-start | bytes 835592 | tf_op jit(solution)/shard_map/ppermute | solution.py:216
  22.7 1.7 %shard_map.52 = (f32[272,256]{1,0:T(8,128)S(1)}, bf16[272,256]{1,0:T(8,128)(2,1)S(1)}) custom-call(bf16[1024,128]{1,0:T(8,128)(2,1)S(1)} %collective-permute-done.near_ref.theirs_ref, bf16[1088,2304]{1,0:T(8,128)(2,1)S(1)} %shard_map.48.lhs_ref, bf16[1024,128]{1,0:T(8,128)(2,1)S(1)} %collective-permute-done.7.theirs2_ref, ...), custom_call_target="tpu_custom_call" | custom-call | flops 5000000000 | bytes 15000000 | tf_op jit(solution)/shard_map/pallas_call | solution.py:331
  24.4 2.7 %collective-permute-start.8 = (bf16[272,256]{1,0:T(8,128)(2,1)S(1)}, bf16[272,256]{1,0:T(8,128)(2,1)S(1)}, u32[]{:S(2)}, u32[]{:S(2)}) collective-permute-start(bf16[272,256]{1,0:T(8,128)(2,1)S(1)} %get-tuple-element.19), channel_id=1, source_target_pairs={{0,2},{1,3},{2,0},{3,1},{4,6},{5,7},{6,4},{7,5},{8,10},{9,11},{10,... | collective-permute-start | bytes 417800 | tf_op jit(solution)/shard_map/ppermute | solution.py:216
  27.1 0.4 collective-permute-start.11
  27.5 5.2 %collective-permute-done.8.refs_1_ = bf16[272,256]{1,0:T(8,128)(2,1)S(1)} collective-permute-done((bf16[272,256]{1,0:T(8,128)(2,1)S(1)}, bf16[272,256]{1,0:T(8,128)(2,1)S(1)}, u32[]{:S(2)}, u32[]{:S(2)}) %collective-permute-start.8) | collective-permute-done | bytes 139296 | tf_op jit(solution)/shard_map/ppermute | solution.py:216
  32.7 0.9 %collective-permute-done.5.refs_1_ = bf16[544,256]{1,0:T(8,128)(2,1)S(1)} collective-permute-done((bf16[544,256]{1,0:T(8,128)(2,1)S(1)}, bf16[544,256]{1,0:T(8,128)(2,1)S(1)}, u32[]{:S(2)}, u32[]{:S(2)}) %collective-permute-start.5) | collective-permute-done | bytes 278560 | tf_op jit(solution)/shard_map/ppermute | solution.py:216
  33.7 2.6 %collective-permute-start.9 = (bf16[272,256]{1,0:T(8,128)(2,1)S(1)}, bf16[272,256]{1,0:T(8,128)(2,1)S(1)}, u32[]{:S(2)}, u32[]{:S(2)}) collective-permute-start(bf16[272,256]{1,0:T(8,128)(2,1)S(1)} %add_convert_fusion.1), channel_id=1, source_target_pairs={{0,2},{1,3},{2,0},{3,1},{4,6},{5,7},{6,4},{7,5},{8,10},{9,11},{10,... | collective-permute-start | bytes 417800 | tf_op jit(solution)/shard_map/ppermute | solution.py:216
  36.3 5.6 %collective-permute-done.11.refs_4_ = bf16[272,256]{1,0:T(8,128)(2,1)S(1)} collective-permute-done((bf16[272,256]{1,0:T(8,128)(2,1)S(1)}, bf16[272,256]{1,0:T(8,128)(2,1)S(1)}, u32[]{:S(2)}, u32[]{:S(2)}) %collective-permute-start.11) | collective-permute-done | bytes 139296 | tf_op jit(solution)/shard_map/ppermute | solution.py:216
  41.9 1.5 %shard_map.53.refs_3_ = f32[3,65,1024]{2,1,0:T(8,128)} custom-call(s32[3]{0:T(128)S(1)} %copy-done.2, f32[272,256]{1,0:T(8,128)S(1)} %get-tuple-element.22.refs_0_, bf16[272,256]{1,0:T(8,128)(2,1)S(1)} %collective-permute-done.8.refs_1_, f32[272,256]{1,0:T(8,128)S(1)} %get-tuple-element.23.refs_2_, bf16[544,256]{1,0:T(8,128)(2,1)S(1)} %collective-permute-done.10.refs_3_, ...), custom_call_target="tpu_custom_call" | custom-call | flops 1000000000 | bytes 3000000 | tf_op jit(solution)/shard_map/pallas_call | solution.py:362
  43.4 0.9 %collective-permute-done.9.refs_2_ = bf16[272,256]{1,0:T(8,128)(2,1)S(1)} collective-permute-done((bf16[272,256]{1,0:T(8,128)(2,1)S(1)}, bf16[272,256]{1,0:T(8,128)(2,1)S(1)}, u32[]{:S(2)}, u32[]{:S(2)}) %collective-permute-start.9) | collective-permute-done | bytes 139296 | tf_op jit(solution)/shard_map/ppermute | solution.py:216
  44.3 1.4 %shard_map.54 = f32[3,65,1024]{2,1,0:T(8,128)} custom-call(s32[3]{0:T(128)S(1)} %copy-done.2, f32[272,256]{1,0:T(8,128)S(1)} %get-tuple-element.15.refs_0_, bf16[544,256]{1,0:T(8,128)(2,1)S(1)} %collective-permute-done.5.refs_1_, bf16[272,256]{1,0:T(8,128)(2,1)S(1)} %collective-permute-done.9.refs_2_, ...), custom_call_target="tpu_custom_call", output_to_operand_aliasing={{}: (4, {})} | custom-call | flops 1000000000 | bytes 3000000 | tf_op jit(solution)/shard_map/pallas_call | solution.py:362
  (9 shorter events, 0.1 us)
Async XLA Ops:
  0.0 10.1 %copy-start.2 = (s32[3]{0:T(128)S(1)}, s32[3]{0:T(128)}, u32[]{:S(2)}) copy-start(s32[3]{0:T(128)} %masks_hbm.3) | copy-start | bytes 40
  2.3 10.4 %collective-permute-start.3 = (bf16[1024,128]{1,0:T(8,128)(2,1)}, bf16[1024,128]{1,0:T(8,128)(2,1)S(1)}, u32[]{:S(2)}, u32[]{:S(2)}) collective-permute-start(bf16[1024,128]{1,0:T(8,128)(2,1)} %shard_map.46.white_ref), channel_id=1, source_target_pairs={{0,28},{4,24},{8,20},{12,16},{16,12},{20,8},{24,4},{28,0},{1,29},{... | collective-permute-start | bytes 786440 | tf_op jit(solution)/shard_map/ppermute | solution.py:216
  5.7 11.1 %collective-permute-start.6 = (bf16[1024,128]{1,0:T(8,128)(2,1)}, bf16[1024,128]{1,0:T(8,128)(2,1)S(1)}, u32[]{:S(2)}, u32[]{:S(2)}) collective-permute-start(bf16[1024,128]{1,0:T(8,128)(2,1)} %shard_map.46.white_ref), channel_id=1, source_target_pairs={{0,1},{1,0},{2,3},{3,2},{4,5},{5,4},{6,7},{7,6},{8,9},{9,8},{10,11... | collective-permute-start | bytes 786440 | tf_op jit(solution)/shard_map/ppermute | solution.py:216
  7.3 2.8 %collective-permute-start = (bf16[1024,128]{1,0:T(8,128)(2,1)}, bf16[1024,128]{1,0:T(8,128)(2,1)S(1)}, u32[]{:S(2)}, u32[]{:S(2)}) collective-permute-start(bf16[1024,128]{1,0:T(8,128)(2,1)} %shard_map.46.white_ref), channel_id=1, source_target_pairs={{0,4},{4,0},{8,12},{12,8},{16,20},{20,16},{24,28},{28,24},{1,5},{5... | collective-permute-start | bytes 786440 | tf_op jit(solution)/shard_map/ppermute | solution.py:216
  7.7 0.9 %copy-start = (bf16[1024,128]{1,0:T(8,128)(2,1)S(1)}, bf16[1024,128]{1,0:T(8,128)(2,1)}, u32[]{:S(2)}) copy-start(bf16[1024,128]{1,0:T(8,128)(2,1)} %shard_map.46.white_ref) | copy-start | bytes 786436
  8.6 1.5 %copy-start.1 = (bf16[1024,128]{1,0:T(8,128)(2,1)S(1)}, bf16[1024,128]{1,0:T(8,128)(2,1)}, u32[]{:S(2)}) copy-start(bf16[1024,128]{1,0:T(8,128)(2,1)} %shard_map.46.white_ref) | copy-start | bytes 786436
  10.3 8.9 %collective-permute-start.1 = (bf16[1024,128]{1,0:T(8,128)(2,1)S(1)}, bf16[1024,128]{1,0:T(8,128)(2,1)S(1)}, u32[]{:S(2)}, u32[]{:S(2)}) collective-permute-start(bf16[1024,128]{1,0:T(8,128)(2,1)S(1)} %shard_map.47), channel_id=1, source_target_pairs={{0,8},{4,12},{8,0},{12,4},{16,24},{20,28},{24,16},{28,20},{1,9},{5... | collective-permute-start | bytes 786440 | tf_op jit(solution)/shard_map/ppermute | solution.py:216
  10.9 8.3 %collective-permute-start.2 = (bf16[1024,128]{1,0:T(8,128)(2,1)S(1)}, bf16[1024,128]{1,0:T(8,128)(2,1)S(1)}, u32[]{:S(2)}, u32[]{:S(2)}) collective-permute-start(bf16[1024,128]{1,0:T(8,128)(2,1)S(1)} %shard_map.47), channel_id=1, source_target_pairs={{0,16},{4,20},{8,24},{12,28},{16,0},{20,4},{24,8},{28,12},{1,17},{... | collective-permute-start | bytes 786440 | tf_op jit(solution)/shard_map/ppermute | solution.py:216
  14.3 12.8 %collective-permute-start.10 = (bf16[544,256]{1,0:T(8,128)(2,1)S(1)}, bf16[544,256]{1,0:T(8,128)(2,1)S(1)}, u32[]{:S(2)}, u32[]{:S(2)}) collective-permute-start(bf16[544,256]{1,0:T(8,128)(2,1)S(1)} %get-tuple-element.17), channel_id=1, source_target_pairs={{0,1},{1,0},{2,3},{3,2},{4,5},{5,4},{6,7},{7,6},{8,9},{9,8},{10,11... | collective-permute-start | bytes 835592 | tf_op jit(solution)/shard_map/ppermute | solution.py:216
  16.8 5.9 %collective-permute-start.7 = (bf16[1024,128]{1,0:T(8,128)(2,1)S(1)}, bf16[1024,128]{1,0:T(8,128)(2,1)S(1)}, u32[]{:S(2)}, u32[]{:S(2)}) collective-permute-start(bf16[1024,128]{1,0:T(8,128)(2,1)S(1)} %collective-permute-done.6.white_ref), channel_id=1, source_target_pairs={{0,4},{4,0},{8,12},{12,8},{16,20},{20,16},{24,28},{28,24},{1,5},{5... | collective-permute-start | bytes 786440 | tf_op jit(solution)/shard_map/ppermute | solution.py:216
  16.8 2.4 %collective-permute-start.4 = (bf16[1024,128]{1,0:T(8,128)(2,1)S(1)}, bf16[1024,128]{1,0:T(8,128)(2,1)S(1)}, u32[]{:S(2)}, u32[]{:S(2)}) collective-permute-start(bf16[1024,128]{1,0:T(8,128)(2,1)S(1)} %collective-permute-done.3.theirs_ref), channel_id=1, source_target_pairs={{0,4},{4,0},{8,12},{12,8},{16,20},{20,16},{24,28},{28,24},{1,5},{5... | collective-permute-start | bytes 786440 | tf_op jit(solution)/shard_map/ppermute | solution.py:216
  21.0 12.7 %collective-permute-start.5 = (bf16[544,256]{1,0:T(8,128)(2,1)S(1)}, bf16[544,256]{1,0:T(8,128)(2,1)S(1)}, u32[]{:S(2)}, u32[]{:S(2)}) collective-permute-start(bf16[544,256]{1,0:T(8,128)(2,1)S(1)} %get-tuple-element.16), channel_id=1, source_target_pairs={{0,1},{1,0},{2,3},{3,2},{4,5},{5,4},{6,7},{7,6},{8,9},{9,8},{10,11... | collective-permute-start | bytes 835592 | tf_op jit(solution)/shard_map/ppermute | solution.py:216
  24.4 8.3 %collective-permute-start.8 = (bf16[272,256]{1,0:T(8,128)(2,1)S(1)}, bf16[272,256]{1,0:T(8,128)(2,1)S(1)}, u32[]{:S(2)}, u32[]{:S(2)}) collective-permute-start(bf16[272,256]{1,0:T(8,128)(2,1)S(1)} %get-tuple-element.19), channel_id=1, source_target_pairs={{0,2},{1,3},{2,0},{3,1},{4,6},{5,7},{6,4},{7,5},{8,10},{9,11},{10,... | collective-permute-start | bytes 417800 | tf_op jit(solution)/shard_map/ppermute | solution.py:216
  27.1 14.7 %collective-permute-start.11 = (bf16[272,256]{1,0:T(8,128)(2,1)S(1)}, bf16[272,256]{1,0:T(8,128)(2,1)S(1)}, u32[]{:S(2)}, u32[]{:S(2)}) collective-permute-start(bf16[272,256]{1,0:T(8,128)(2,1)S(1)} %add_convert_fusion), channel_id=1, source_target_pairs={{0,2},{1,3},{2,0},{3,1},{4,6},{5,7},{6,4},{7,5},{8,10},{9,11},{10,... | collective-permute-start | bytes 417800 | tf_op jit(solution)/shard_map/ppermute | solution.py:216
  33.7 10.6 %collective-permute-start.9 = (bf16[272,256]{1,0:T(8,128)(2,1)S(1)}, bf16[272,256]{1,0:T(8,128)(2,1)S(1)}, u32[]{:S(2)}, u32[]{:S(2)}) collective-permute-start(bf16[272,256]{1,0:T(8,128)(2,1)S(1)} %add_convert_fusion.1), channel_id=1, source_target_pairs={{0,2},{1,3},{2,0},{3,1},{4,6},{5,7},{6,4},{7,5},{8,10},{9,11},{10,... | collective-permute-start | bytes 417800 | tf_op jit(solution)/shard_map/ppermute | solution.py:216
